TPU v7x, 128 devices: a whole 4x4x4 slice. The times are simulated.
128 devices in a mesh: row: 16 (over x_lo, y, core), col: 8 (over z, x_hi).
Axes of the slice: x: 4 (x_hi: 2, x_lo: 2; x = x_hi * 2 + x_lo), y: 4, z: 4, core: 2. Of those that a mesh axis runs over, the one named last changes fastest.
Arguments:
- ortho_in: bfloat16 [7168, 9216], P(('row', 'col')), may hold values from -6 to 6
Outputs:
- next_iterate: bfloat16 [7168, 9216], P(('row', 'col'))
All inputs are finite; a program needn't handle non-finite values.
Results may differ from a plain program's by a relative error of at most 0.024.
Values may be sent and summed in bfloat16 or wider, within the bound.
A program may use at most 128 MiB of HBM per device.

v0:
```python
import math

import jax
import jax.numpy as jnp
from jax import lax
from jax.sharding import PartitionSpec as P

coef_a = 3.4445
coef_b = -4.775
coef_c = 2.0315


def per_device(ortho_in):
    tile = lax.all_to_all(ortho_in, "col", split_axis=1, concat_axis=0, tiled=True)
    tile_rows = tile.shape[0]
    tile_cols = tile.shape[1]
    full_rows = tile_rows * lax.axis_size("row")
    full_cols = tile_cols * lax.axis_size("col")
    inv_square = 1.0 / (math.sqrt(full_rows) + math.sqrt(full_cols)) ** 2
    panel = lax.all_gather(tile, "row", axis=0, tiled=True)
    partial_gram = lax.dot_general(
        tile, panel, (((1,), (1,)), ((), ())), preferred_element_type=jnp.float32
    )
    gram_total = lax.psum(partial_gram.astype(jnp.bfloat16), "col").astype(jnp.float32)
    gram = (gram_total * inv_square).astype(jnp.bfloat16)
    first_f = jnp.dot(gram, panel, preferred_element_type=jnp.float32)
    first_prod = first_f.astype(jnp.bfloat16)
    second_prod = jnp.dot(
        gram,
        lax.all_gather(first_prod, "row", axis=0, tiled=True),
        preferred_element_type=jnp.float32,
    )
    iterate = (
        coef_a * tile.astype(jnp.float32)
        + coef_b * first_prod.astype(jnp.float32)
        + coef_c * second_prod
    )
    result_tile = iterate.astype(jnp.bfloat16)
    return lax.all_to_all(result_tile, "col", split_axis=0, concat_axis=1, tiled=True)


def solution(mesh):
    in_specs = (P(("row", "col"), None),)
    out_specs = P(("row", "col"), None)
    return jax.shard_map(
        per_device, mesh=mesh, in_specs=in_specs, out_specs=out_specs, check_vma=False
    )
```

profile of v0, /device:TPU:1, one launch (start us, length us, event | category | flops | bytes accessed | tf_op | source)
XLA Modules:
  0.0 553.3 jit_solution(15117017379384241305)
XLA Ops:
  6.5 0.0 all-gather.3.cloned.1.call-start
  6.5 1.3 copy.7
  7.8 24.3 %all_to_all.38 = bf16[56,8,1152]{2,0,1:T(8,128)(2,1)} all-to-all(bf16[56,8,1152]{2,0,1:T(8,128)(2,1)S(1)} %bitcast.19), channel_id=1, replica_groups=mesh['row'=16,'col'=8] {'col'}, dimensions={1} | all-to-all | bytes 2064384 | tf_op jit(solution)/shard_map/all_to_all | solution.py:14
  32.2 0.0 all-gather.3.cloned.1.call-update
  32.2 0.0 all-reduce.2.cloned.1.call-start
  32.3 89.5 %all-gather.3.cloned.1.call-done = bf16[7168,1152]{1,0:T(8,128)(2,1)} async-done(((bf16[448,1152]{1,0:T(8,128)(2,1)}), bf16[7168,1152]{1,0:T(8,128)(2,1)}) %all-gather.3.cloned.1.call-update) | async-done | bytes 16515088 | tf_op jit(solution)/shard_map/all_gather | solution.py:20
  121.8 14.0 %convolution_convert_fusion = bf16[448,7168]{1,0:T(8,128)(2,1)} fusion(bf16[448,1152]{1,0:T(8,128)(2,1)} %bitcast.16, bf16[7168,1152]{1,0:T(8,128)(2,1)} %all-gather.3.cloned.1.call-done), kind=kOutput, calls=%fused_computation.1 | convolution fusion | flops 7401963520 | bytes 23969792 | tf_op jit(solution)/shard_map/dot_general | solution.py:21
  135.8 0.0 all-reduce.2.cloned.1.call-update
  135.8 0.0 copy-start
  135.8 0.0 all-gather.5.cloned.1.call-start
  135.9 268.6 %all-reduce.2.cloned.1.call-done = bf16[448,7168]{1,0:T(8,128)(2,1)} async-done(((bf16[448,7168]{1,0:T(8,128)(2,1)}), bf16[448,7168]{1,0:T(8,128)(2,1)}) %all-reduce.2.cloned.1.call-update) | async-done | bytes 6422544 | tf_op jit(solution)/shard_map/psum | solution.py:24
  404.4 14.0 %fusion.5 = bf16[448,1152]{1,0:T(8,128)(2,1)} fusion(bf16[7168,1152]{1,0:T(8,128)(2,1)} %all-gather.3.cloned.1.call-done, bf16[448,7168]{1,0:T(8,128)(2,1)} %all-reduce.2.cloned.1.call-done), kind=kOutput, calls=%fused_computation.7 | convolution fusion | flops 7408902144 | bytes 23969792 | tf_op jit(solution)/shard_map/dot_general | solution.py:26
  418.4 0.0 all-gather.5.cloned.1.call-update
  418.5 90.8 %all-gather.5.cloned.1.call-done = bf16[7168,1152]{1,0:T(8,128)(2,1)} async-done(((bf16[448,1152]{1,0:T(8,128)(2,1)}), bf16[7168,1152]{1,0:T(8,128)(2,1)}) %all-gather.5.cloned.1.call-update) | async-done | bytes 16515088 | tf_op jit(solution)/shard_map/all_gather | solution.py:30
  509.3 0.0 copy-done
  509.3 13.7 %fusion.4 = bf16[448,1152]{1,0:T(8,128)(2,1)S(1)} fusion(bf16[7168,1152]{1,0:T(8,128)(2,1)} %all-gather.5.cloned.1.call-done, bf16[448,7168]{1,0:T(8,128)(2,1)} %all-reduce.2.cloned.1.call-done, bf16[448,1152]{1,0:T(8,128)(2,1)} %fusion.5, bf16[448,1152]{1,0:T(8,128)(2,1)S(1)} %bitcast.17), kind=kOutput, calls=%fused_computation.6 | convolution fusion | flops 7412514816 | bytes 26034176 | tf_op jit(solution)/shard_map/dot_general | solution.py:28
  523.0 22.7 %all_to_all.39 = bf16[8,56,1152]{2,1,0:T(8,128)(2,1)S(1)} all-to-all(bf16[8,56,1152]{2,1,0:T(8,128)(2,1)S(1)} %bitcast.21), channel_id=1, replica_groups=mesh['row'=16,'col'=8] {'col'}, dimensions={0} | all-to-all | bytes 2064384 | tf_op jit(solution)/shard_map/all_to_all | solution.py:39
  545.7 1.1 copy.5
Async XLA Ops:
  6.5 115.3 %all-gather.3.cloned.1.call-start = ((), (), s32[]{:S(2)}) async-start(), calls=%async_computation.2 | async-start | bytes 17547264 | tf_op jit(solution)/shard_map/all_gather | solution.py:20
  32.2 372.2 %all-reduce.2.cloned.1.call-start = ((), (), s32[]{:S(2)}) async-start(), calls=%async_computation.3 | async-start | bytes 12845056 | tf_op jit(solution)/shard_map/psum | solution.py:24
  135.8 373.5 %copy-start = (bf16[56,8,1152]{2,0,1:T(8,128)(2,1)S(1)}, bf16[56,8,1152]{2,0,1:T(8,128)(2,1)}, u32[]{:S(2)}) copy-start(bf16[56,8,1152]{2,0,1:T(8,128)(2,1)} %all_to_all.38) | copy-start | bytes 3096580
  135.8 373.5 %all-gather.5.cloned.1.call-start = ((), (), s32[]{:S(2)}) async-start(), calls=%async_computation.4 | async-start | bytes 17547264 | tf_op jit(solution)/shard_map/all_gather | solution.py:30
Sparse Core Ops, SparseCore 0:
  32.3 89.4 all-gather.2
  135.9 268.4 all-reduce.1
  418.6 90.6 all-gather.4
where the time goes:
time: 554 us; the launch traced here: 553 us
  waiting for transfers between devices  449 us (81%)
  blocking collectives  47 us (8%)
  matrix products  41.7 us (8%)
  between operations  13.1 us (2%)
    psum x1, waiting for transfers between devices, per_device(): lax.psum(partial_gram.astype(jnp.bfloat16), 'col').astype(jnp.float32)  269 us
    all_gather x1, waiting for transfers between devices, per_device(): lax.all_gather(first_prod, 'row', axis=0, tiled=True)  90.8 us
    all_gather x1, waiting for transfers between devices, per_device(): panel = lax.all_gather(tile, 'row', axis=0, tiled=True)  89.5 us
    all_to_all x1, blocking collectives, per_device(): lax.all_to_all(ortho_in, 'col', split_axis=1, concat_axis=0, tiled=True)  24.3 us
    all_to_all x1, blocking collectives, per_device(): lax.all_to_all(result_tile, 'col', split_axis=0, concat_axis=1, tiled=True)  22.7 us
    dot_general x1, matrix products, per_device(): first_f = jnp.dot(gram, panel, preferred_element_type=jnp.float32)  14 us
    dot_general x1, matrix products, per_device(): lax.dot_general(tile, panel, (((1,), (1,)), ((), ())), preferred_element_...  14 us
    dot_general x1, matrix products, per_device(): jnp.dot(gram, lax.all_gather(first_prod, 'row', axis=0, tiled=True), pref...  13.7 us
  transfers between devices with their start and end apart: 3, of which 3 were waited for; matrix products, arithmetic and copies ran while one was open for 0% of the time, Pallas kernels for 0%

commit v1 on v0

v1 whole, which is shorter than its diff:
```python
import functools
import math

import jax
import jax.numpy as jnp
from jax import lax
from jax.experimental import pallas as pl
from jax.experimental.pallas import tpu as pltpu
from jax.sharding import PartitionSpec as P

coef_a = 3.4445
coef_b = -4.775
coef_c = 2.0315

MESH = pl.DeviceIdType.MESH
F32 = jnp.float32
BF16 = jnp.bfloat16

ROWS = 112
HALF = 56
PW = 1152
BLK = 1792
CUT = 512
HB = BLK // 2


def kernel(
    inv_square,
    xin,
    out,
    sb,
    ex,
    stage,
    xp,
    yp,
    pbuf,
    rbuf,
    rx,
    gb,
    zacc,
    oin,
    sem_misc,
    sem_a2a,
    sem_ag,
    sem_agd,
    sem_rs,
    sem_send,
    sem_g,
    sem_back,
):
    row, col = lax.axis_index("row"), lax.axis_index("col")
    k = row % 2
    y = (row // 2) % 4
    x = (col % 2) * 2 + row // 8
    z = col // 2
    r_x = ((x + 1) // 2) % 2
    c_x = x // 2
    rho = r_x * 4 + y

    def dev(xx, yy, zz, kk):
        return (((xx % 2) * 4 + yy) * 2 + kk, zz * 2 + xx // 2)

    x_row = x + 1 - 2 * (x % 2)
    x_col = 3 - x
    ring = {1: dev(x, (y + 1) % 4, z, k), -1: dev(x, (y + 3) % 4, z, k)}
    pair = dev(x_row, y, z, k)
    zring = {1: dev(x, y, (z + 1) % 4, k), -1: dev(x, y, (z + 3) % 4, k)}
    cpair = dev(x_col, y, z, k)
    sib = dev(x, y, z, 1 - k)
    same = k == c_x
    x_far = x + (x_col - x) * (k + c_x - 2 * k * c_x)
    far = [dev(x_far, y, (z + d) % 4, c_x) for d in range(4)]

    def rdma(src, dst, ssem, rsem, device):
        return pltpu.make_async_remote_copy(
            src_ref=src,
            dst_ref=dst,
            send_sem=ssem,
            recv_sem=rsem,
            device_id=device,
            device_id_type=MESH,
        )

    def wait_bytes(ref, sem):
        pltpu.make_async_copy(ref, ref, sem).wait()

    def rows_of(slot):
        return pl.ds(pl.multiple_of(slot * ROWS, 16), ROWS)

    barrier = pltpu.get_barrier_semaphore()
    for d in (ring[1], ring[-1], pair, zring[1], zring[-1], cpair, sib, *far[1:]):
        pl.semaphore_signal(barrier, inc=1, device_id=d, device_id_type=MESH)

    @pl.when(jnp.logical_not(same))
    def _():
        pl.semaphore_signal(barrier, inc=1, device_id=far[0], device_id_type=MESH)

    half = 4 * PW
    mine = pl.ds(pl.multiple_of(k * half, 128), half)
    other = pl.ds(pl.multiple_of((1 - k) * half, 128), half)
    my_rows = pl.ds(pl.multiple_of(k * HALF, 8), HALF)
    other_rows = pl.ds(pl.multiple_of((1 - k) * HALF, 8), HALF)
    sb[...] = xin[:, other].astype(F32)
    ex[my_rows, :] = xin[:, mine].astype(F32)
    pl.semaphore_wait(barrier, 10 + k + c_x - 2 * k * c_x)
    swap = rdma(sb, ex.at[my_rows], sem_misc.at[0], sem_misc.at[1], sib)
    swap.start()
    swap.wait()
    for i in range(4):
        stage[i] = ex[:, i * PW : (i + 1) * PW].astype(BF16)

    my_slot = c_x * 8 + rho
    for d in (0, 1, 3, 2):
        dst = xp.at[z, rows_of(my_slot)]
        if d == 0:

            @pl.when(same)
            def _():
                pltpu.make_async_copy(stage.at[z], dst, sem_a2a.at[z]).start()

            @pl.when(jnp.logical_not(same))
            def _():
                rdma(
                    stage.at[z], dst, sem_send.at[14], sem_a2a.at[z], far[0]
                ).start()

        else:
            rdma(
                stage.at[(z + d) % 4], dst, sem_send.at[14 + d], sem_a2a.at[z], far[d]
            ).start()

    def wait_a2a(u):
        wait_bytes(xp.at[u, rows_of(k * 8 + rho)], sem_a2a.at[u])

    def slot_of(s, e):
        rr = r_x if s == 0 else 1 - r_x
        return k * 8 + rr * 4 + (y + e + 4) % 4

    class Gather:
        def __init__(self, buf, base, t, u):
            self.buf, self.base, self.t, self.u = buf, base, t, u
            self.par = 1 if t % 2 == 0 else -1

        def piece(self, s, e, part="AB"):
            ref = self.buf.at[self.u, rows_of(slot_of(s, e))]
            if part == "A":
                ref = ref.at[:, pl.ds(0, CUT)]
            elif part == "B":
                ref = ref.at[:, pl.ds(CUT, PW - CUT)]
            return ref

        IDX = {
            (0, -1, "AB"): 0,
            (0, 1, "AB"): 1,
            (0, 2, "AB"): 2,
            (1, 0, "AB"): 3,
            (1, -1, "A"): 4,
            (1, -1, "B"): 5,
            (1, 1, "A"): 6,
            (1, 1, "B"): 7,
            (1, 2, "A"): 8,
            (1, 2, "B"): 9,
        }

        def rsem(self, *key):
            return sem_ag.at[self.base * 4 + self.t, self.IDX[key]]

        def send(self, s, e, part, device, key):
            ref = self.piece(s, e, part)
            rdma(
                ref, ref, sem_send.at[self.base * 4 + self.t], self.rsem(*key), device
            ).start()

        def to_sib(self, s, e):
            ref = self.piece(s, e)
            i = self.base * 4 + self.t
            rdma(ref, ref, sem_agd.at[i, 0], sem_agd.at[i, 1], sib).start()

        def wait(self, s, e, part):
            wait_bytes(self.piece(s, e, part), self.rsem(s, e, part))

        def own(self):
            self.send(0, 0, "AB", ring[1], (0, -1, "AB"))
            self.send(0, 0, "AB", ring[-1], (0, 1, "AB"))
            self.send(0, 0, "AB", pair, (1, 0, "AB"))
            self.to_sib(0, 0)

        def level1(self):
            self.wait(1, 0, "AB")
            self.send(1, 0, "B", ring[1], (1, -1, "B"))
            self.send(1, 0, "B", ring[-1], (1, 1, "B"))
            self.to_sib(1, 0)
            for e in (-1, 1):
                self.wait(0, e, "AB")
                if e == -self.par:
                    self.send(0, e, "AB", ring[self.par], (0, 2, "AB"))
                self.send(0, e, "A", pair, (1, e, "A"))
                self.to_sib(0, e)

        def level2(self):
            self.wait(1, -self.par, "B")
            self.send(1, -self.par, "B", ring[self.par], (1, 2, "B"))
            self.wait(0, 2, "AB")
            self.send(0, 2, "A", pair, (1, 2, "A"))
            self.to_sib(0, 2)

        def level3(self):
            self.wait(1, self.par, "B")
            for e in (-1, 1):
                self.wait(1, e, "A")
                self.to_sib(1, e)
            self.wait(1, 2, "B")
            self.wait(1, 2, "A")
            self.to_sib(1, 2)

        def all_here(self):
            i = self.base * 4 + self.t
            ref = self.buf.at[self.u, pl.ds(pl.multiple_of((1 - k) * HB, 16), HB)]
            wait_bytes(ref, sem_agd.at[i, 1])

        def sent(self):
            i = self.base * 4 + self.t
            wait_bytes(self.buf.at[self.u, pl.ds(0, 7 * ROWS)], sem_send.at[i])
            wait_bytes(self.buf.at[self.u, pl.ds(0, HB)], sem_agd.at[i, 0])

    def tile():
        return jnp.concatenate(
            [xp[v, rows_of(k * 8 + rho), :] for v in range(4)], axis=0
        )

    def half_cols(c):
        return pl.ds(c * HB, HB)

    def partial_gram(u, c):
        for n in range(2):
            cols = pl.ds(c * HB + n * 448, 448)
            part = lax.dot_general(
                tile(),
                xp[u, cols, :],
                (((1,), (1,)), ((), ())),
                preferred_element_type=F32,
            ).astype(BF16)
            for v in range(4):
                pbuf[u, v, :, cols] = part[v * ROWS : (v + 1) * ROWS]

    def rs_send(src, dst, u, c, i, device):
        rdma(src, dst, sem_send.at[8 + u], sem_rs.at[u * 2 + c, i], device).start()

    def rs1(u, c):
        s = 1 if c == 0 else -1
        h = half_cols(c)
        rs_send(
            pbuf.at[u, (z + 2) % 4, :, h], rbuf.at[u, 0, :, h], u, c, 0, zring[s]
        )
        rs_send(
            pbuf.at[u, (z + 4 - s) % 4, :, h], rbuf.at[u, 1, :, h], u, c, 1, zring[-s]
        )

    def rs2(u, c):
        s = 1 if c == 0 else -1
        h = half_cols(c)
        v = (z + 4 + s) % 4
        wait_bytes(rbuf.at[u, 0, :, h], sem_rs.at[u * 2 + c, 0])
        pbuf[u, v, :, h] = (
            pbuf[u, v, :, h].astype(F32) + rbuf[u, 0, :, h].astype(F32)
        ).astype(BF16)
        rs_send(pbuf.at[u, v, :, h], rbuf.at[u, 2, :, h], u, c, 2, zring[s])

    def rs3(u, c):
        h = half_cols(c)
        wait_bytes(rbuf.at[u, 1, :, h], sem_rs.at[u * 2 + c, 1])
        wait_bytes(rbuf.at[u, 2, :, h], sem_rs.at[u * 2 + c, 2])
        pbuf[u, z, :, h] = (
            pbuf[u, z, :, h].astype(F32)
            + rbuf[u, 1, :, h].astype(F32)
            + rbuf[u, 2, :, h].astype(F32)
        ).astype(BF16)
        rs_send(pbuf.at[u, z, :, h], rx.at[u, :, h], u, c, 3, cpair)

    def rs4(u, c):
        h = half_cols(c)
        wait_bytes(rx.at[u, :, h], sem_rs.at[u * 2 + c, 3])
        total = pbuf[u, z, :, h].astype(F32) + rx[u, :, h].astype(F32)
        gb[z, u, :, h] = (total * inv_square).astype(BF16)

    ax = [Gather(xp, 0, u, u) for u in range(4)]
    wait_a2a(0)
    ax[0].own()
    for u in range(4):
        ax[u].level1()
        if u == 0:
            wait_a2a(1)
        if u < 3:
            ax[u + 1].own()
        if u > 0:
            rs2(u - 1, 0)
            rs2(u - 1, 1)
        ax[u].level2()
        if u > 0:
            rs3(u - 1, 0)
            rs3(u - 1, 1)
        ax[u].level3()
        if u == 0:
            wait_a2a(2)
            wait_a2a(3)
        if u > 0:
            rs4(u - 1, 0)
            rs4(u - 1, 1)
        ax[u].all_here()
        for c in range(2):
            partial_gram(u, c)
            rs1(u, c)
    for f in (rs2, rs3, rs4):
        for c in range(2):
            f(3, c)

    def u_of(w):
        return w + c_x * (3 - 2 * w)

    def gref(e, w, h=None):
        ref = gb.at[(z + e + 4) % 4, u_of(w)]
        return ref if h is None else ref.at[:, half_cols(h)]

    def g_send(e, w, device, i, h=None):
        rdma(gref(e, w, h), gref(e, w, h), sem_send.at[12], sem_g.at[i], device).start()

    def g_wait(e, w, i, h=None):
        wait_bytes(gref(e, w, h), sem_g.at[i])

    for w in range(3):
        g_send(0, w, zring[1], w)
        g_send(0, w, zring[-1], 3 + w)

    ay = [Gather(yp, 1, t, (z + e) % 4) for t, e in enumerate((0, 3, 1, 2))]

    def first_prod(t):
        v = ay[t].u
        acc = jnp.dot(gb[v, 0], xp[0], preferred_element_type=F32)
        zacc[pl.ds(0, ROWS), :] = acc
        for u in range(1, 4):
            zacc[pl.ds(0, ROWS), :] += jnp.dot(
                gb[v, u], xp[u], preferred_element_type=F32
            )
        yp[v, rows_of(k * 8 + rho), :] = zacc[pl.ds(0, ROWS), :].astype(BF16)

    def second_prod(t):
        v = ay[t].u
        g = jnp.concatenate([gb[i, v] for i in range(4)], axis=0)
        for n in range(3):
            cols = pl.ds(n * 384, 384)
            term = jnp.dot(g, yp[v, :, cols], preferred_element_type=F32)
            if t == 0:
                zacc[:, cols] = term
            else:
                zacc[:, cols] += term

    first_prod(0)
    ay[0].own()

    g_wait(-1, 0, 0)
    g_send(-1, 0, cpair, 10)
    g_send(-1, 0, zring[1], 6)
    g_wait(1, 0, 3)
    g_send(1, 0, cpair, 11)
    ay[0].level1()
    g_wait(-1, 1, 1)
    g_wait(1, 1, 4)
    g_send(1, 1, zring[-1], 7)
    ay[0].level2()
    ay[0].level3()
    g_wait(-1, 2, 2)
    g_send(-1, 2, zring[1], 8, 0)
    g_wait(1, 2, 5)
    g_send(1, 2, zring[-1], 9, 1)
    g_wait(-1, 3, 10)
    first_prod(1)
    ay[1].own()
    g_wait(1, 3, 11)
    first_prod(2)
    ay[1].level1()
    ay[2].own()
    g_wait(2, 0, 6)
    g_send(2, 0, cpair, 12)
    ay[1].level2()
    ay[2].level1()
    g_wait(2, 1, 7)
    g_wait(2, 2, 8, 0)
    g_wait(2, 2, 9, 1)
    g_wait(2, 3, 12)
    first_prod(3)
    ay[3].own()
    ay[1].level3()
    ay[2].level2()
    ay[0].all_here()
    second_prod(0)
    ay[3].level1()
    ay[2].level3()
    ay[1].all_here()
    second_prod(1)
    ay[3].level2()
    ay[2].all_here()
    second_prod(2)
    ay[3].level3()
    ay[3].all_here()
    second_prod(3)

    for d in range(4):
        wait_bytes(stage.at[(z + d) % 4], sem_send.at[14 + d]) if d else None

    @pl.when(jnp.logical_not(same))
    def _():
        wait_bytes(stage.at[z], sem_send.at[14])

    for v in range(4):
        own = rows_of(k * 8 + rho)
        it = (
            coef_a * xp[v, own, :].astype(F32)
            + coef_b * yp[v, own, :].astype(F32)
            + coef_c * zacc[pl.ds(v * ROWS, ROWS), :]
        )
        stage[v] = it.astype(BF16)
    for d in (2, 1, 3, 0):
        src, dst = stage.at[(z + d) % 4], oin.at[z]
        if d == 0:

            @pl.when(same)
            def _():
                pltpu.make_async_copy(src, dst, sem_back.at[z]).start()

            @pl.when(jnp.logical_not(same))
            def _():
                rdma(src, dst, sem_send.at[18], sem_back.at[z], far[0]).start()

        else:
            rdma(src, dst, sem_send.at[18 + d], sem_back.at[z], far[d]).start()
    for v in range(4):
        wait_bytes(oin.at[v], sem_back.at[v])
    for v in range(4):
        ex[:, v * PW : (v + 1) * PW] = oin[v].astype(F32)
    back = rdma(ex.at[other_rows], sb, sem_misc.at[2], sem_misc.at[3], sib)
    back.start()
    out[:, mine] = ex[my_rows, :].astype(BF16)
    back.wait()
    out[:, other] = sb[...].astype(BF16)

    for g in (*ax, *ay):
        g.sent()
    for u in range(4):
        wait_bytes(pbuf.at[u], sem_send.at[8 + u])
    wait_bytes(gb.at[pl.ds(0, 3)], sem_send.at[12])
    for d in range(1, 4):
        wait_bytes(stage.at[(z + d) % 4], sem_send.at[18 + d])

    @pl.when(jnp.logical_not(same))
    def _():
        wait_bytes(stage.at[z], sem_send.at[18])


def solution(mesh):
    def step(ortho_in):
        rows, full_cols = ortho_in.shape
        full_rows = rows * mesh.size
        inv_square = 1.0 / (math.sqrt(full_rows) + math.sqrt(full_cols)) ** 2
        vmem = pltpu.VMEM
        dma = pltpu.SemaphoreType.DMA
        return pl.pallas_call(
            functools.partial(kernel, inv_square),
            name="newton_schulz",
            out_shape=jax.ShapeDtypeStruct((rows, full_cols), BF16),
            in_specs=[pl.BlockSpec(memory_space=pltpu.VMEM)],
            out_specs=pl.BlockSpec(memory_space=pltpu.VMEM),
            scratch_shapes=[
                vmem((HALF, 4 * PW), F32),
                vmem((ROWS, 4 * PW), F32),
                vmem((4, ROWS, PW), BF16),
                vmem((4, BLK, PW), BF16),
                vmem((4, BLK, PW), BF16),
                vmem((4, 4, ROWS, BLK), BF16),
                vmem((4, 3, ROWS, BLK), BF16),
                vmem((4, ROWS, BLK), BF16),
                vmem((4, 4, ROWS, BLK), BF16),
                vmem((4 * ROWS, PW), F32),
                vmem((4, ROWS, PW), BF16),
                dma((4,)),
                dma((4,)),
                dma((8, 10)),
                dma((8, 2)),
                dma((8, 4)),
                dma((22,)),
                dma((13,)),
                dma((4,)),
            ],
            compiler_params=pltpu.CompilerParams(
                collective_id=0,
                has_side_effects=True,
                vmem_limit_bytes=64 * 2**20 - 2**18,
            ),
            cost_estimate=pl.CostEstimate(
                flops=3 * 2 * 448 * 7168 * 1152,
                bytes_accessed=4 * 56 * 9216,
                transcendentals=0,
            ),
        )(ortho_in)

    spec = P(("row", "col"), None)
    return jax.shard_map(
        step, mesh=mesh, in_specs=(spec,), out_specs=spec, check_vma=False
    )
```

time: 554 us -> 258 us (0.47)
  waiting for transfers between devices: 449 us -> 0 us
  Pallas kernels: 0 us -> 256 us
  blocking collectives: 47 us -> 0 us
  matrix products: 41.7 us -> 0 us
  between operations: 13.1 us -> 0.01 us
    psum x1 -> x0, waiting for transfers between devices: 269 us -> none  [per_device(): lax.psum(partial_gram.astype(jnp.bfloat16), 'col').astype(jnp.float32)]
    pallas_call x0 -> x1, Pallas kernels: none -> 256 us  [step(): pl.pallas_call(functools.partial(kernel, inv_square), name='newton_schulz...]
    all_gather x2 -> x0, waiting for transfers between devices: 180 us -> none  [the longest x1 90.8 us: per_device(): lax.all_gather(first_prod, 'row', axis=0, tiled=True)]
    all_to_all x2 -> x0, blocking collectives: 47 us -> none  [the longest x1 24.3 us: per_device(): lax.all_to_all(ortho_in, 'col', split_axis=1, concat_axis=0, tiled=True)]
    dot_general x3 -> x0, matrix products: 41.7 us -> none  [the longest x1 14 us: per_device(): first_f = jnp.dot(gram, panel, preferred_element_type=jnp.float32)]
  transfers between devices with their start and end apart: 3 -> 0, of which waited for: 3 -> 0; matrix products, arithmetic and copies ran while one was open for 0% -> 0% of each run, Pallas kernels for 0% -> 0%
where the time goes in v1:
time: 258 us
  Pallas kernels  256 us (99%)
    pallas_call x1, Pallas kernels, step(): pl.pallas_call(functools.partial(kernel, inv_square), name='newton_schulz...  256 us

profile of v1, /device:TPU:1, one launch (start us, length us, event | category | flops | bytes accessed | tf_op | source)
XLA Modules:
  0.0 258.0 jit_solution(18402712030289142427)
XLA Ops:
  0.0 255.8 %newton_schulz.1 = bf16[56,9216]{1,0:T(8,128)(2,1)} custom-call(bf16[56,9216]{1,0:T(8,128)(2,1)} %xin.1), custom_call_target="tpu_custom_call" | custom-call | flops 22196256768 | bytes 2064384 | tf_op jit(solution)/shard_map/newton_schulz/pallas_call | solution.py:466
  255.8 2.2 copy.3

commit v2 on v0

v2 whole, which is shorter than its diff:
```python
import functools
import math

import jax
import jax.numpy as jnp
from jax import lax
from jax.experimental import pallas as pl
from jax.experimental.pallas import tpu as pltpu
from jax.sharding import PartitionSpec as P

coef_a = 3.4445
coef_b = -4.775
coef_c = 2.0315

MESH = pl.DeviceIdType.MESH
F32 = jnp.float32
BF16 = jnp.bfloat16

ROWS = 112
HALF = 56
PAD = 64
PW = 1152
BLK = 1792
HB = BLK // 2
SIDE = 4 * ROWS
X_PASS = (0, PW, 512)
Y_PASS = ((0, 640, 256), (640, 512, 256))

ORDER = (
    "a0", "x0o", "a1", "x1o", "a2", "a3", "x0m", "x0q", "x0p", "x1m", "x1q", "x1p", "x0r", "x0b",
    "x1r", "x2o", "g00", "x1b", "g10", "x0e", "s00", "x2q", "g01", "x2m", "x1e", "x3o", "s10",
    "x2p", "g11", "t00", "s01", "x2r", "x3q", "x3p", "g20", "w00", "s11", "x3m", "t10", "t01",
    "x2b", "x3r", "x3b", "g30", "w10", "x2e", "s20", "t11", "w01", "x3e", "g21", "s30", "g31",
    "w11", "t20", "s21", "s31", "w20", "t30", "t21", "t31", "h0", "w30", "w21", "h2", "w31", "h3",
    "f0", "i0", "j0", "y10o", "y00o", "y10m", "y10p", "y10q", "i2", "j2", "y00m", "y00q", "y00p",
    "y10r", "y10b", "y00r", "i3", "j3", "f1", "y00b", "y11o", "y10e", "y01o", "f2", "k0", "y00e",
    "y12o", "y11p", "y11q", "y02o", "y11m", "y01q", "y01p", "y01m", "y12q", "y12p", "y11b", "y12m",
    "y11r", "f3", "z10", "z00", "y01r", "y12b", "y02q", "y02m", "y02p", "y13o", "y12r", "y01b",
    "y03o", "y11e", "y02r", "z11", "y13p", "y02b", "y13q", "y12e", "y01e", "y13m", "z12", "z01",
    "y13b", "y03q", "y03m", "y03p", "y02e", "y13r", "z02", "y13e", "y03r", "y03b", "z13", "o1",
    "y03e", "z03", "o0", "v1", "v0",
)


def kernel(
    inv_square,
    xin,
    out,
    xs,
    ain,
    xp,
    yp,
    pbuf,
    rbuf,
    rx,
    gb,
    zacc,
    fin,
    oin,
    sem_a2a,
    sem_ag,
    sem_agd,
    sem_rs,
    sem_g,
    sem_back,
    sem_send,
):
    row, col = lax.axis_index("row"), lax.axis_index("col")
    k = row % 2
    y = (row // 2) % 4
    x = (col % 2) * 2 + row // 8
    z = col // 2
    r_x = ((x + 1) // 2) % 2
    c_x = x // 2

    def dev(xx, yy, zz, kk):
        return (((xx % 2) * 4 + yy) * 2 + kk, zz * 2 + xx // 2)

    x_row = x + 1 - 2 * (x % 2)
    x_col = 3 - x
    ring = {1: dev(x, (y + 1) % 4, z, k), -1: dev(x, (y + 3) % 4, z, k)}
    pair = dev(x_row, y, z, k)
    zring = {1: dev(x, y, (z + 1) % 4, k), -1: dev(x, y, (z + 3) % 4, k)}
    cpair = dev(x_col, y, z, k)
    sib = dev(x, y, z, 1 - k)
    same = k == c_x
    other = k + c_x - 2 * k * c_x
    x_far = x + (x_col - x) * other

    def rdma(src, dst, ssem, rsem, device):
        return pltpu.make_async_remote_copy(
            src_ref=src,
            dst_ref=dst,
            send_sem=ssem,
            recv_sem=rsem,
            device_id=device,
            device_id_type=MESH,
        )

    def wait_bytes(ref, sem):
        pltpu.make_async_copy(ref, ref, sem).wait()

    def rows_at(start, n):
        return pl.ds(pl.multiple_of(start, 16), n)

    def cols_at(start, n):
        return pl.ds(pl.multiple_of(start, 128), n)

    def move(src, dst, ssem, rsem, device, self_too):
        if not self_too:
            rdma(src, dst, ssem, rsem, device).start()
            return

        @pl.when(same)
        def _():
            pltpu.make_async_copy(src, dst, rsem).start()

        @pl.when(jnp.logical_not(same))
        def _():
            rdma(src, dst, ssem, rsem, device).start()

    barrier = pltpu.get_barrier_semaphore()

    def greet(device):
        pl.semaphore_signal(barrier, inc=1, device_id=device, device_id_type=MESH)

    way_in = []
    for d in (0, 1, 3, 2):
        for i in range(2):
            xx, cc = (x, c_x) if i == 0 else (x_col, 1 - c_x)
            zz = (z + d) % 4
            way_in.append((dev(xx, y, zz, c_x), cc, zz, d == 0 and i == 0))
    way_back = []
    for d in (2, 1, 3, 0):
        for i in range(2):
            kk = k if i == 0 else 1 - k
            zz = (z + d) % 4
            way_back.append((dev(x_far, y, zz, kk), zz, kk, d == 0 and i == 0))
    for d in (ring[1], ring[-1], pair, zring[1], zring[-1], cpair, sib):
        greet(d)
    for d, _, _, self_too in way_in + way_back:
        if not self_too:
            greet(d)

    @pl.when(jnp.logical_not(same))
    def _():
        for d, _, _, self_too in way_in + way_back:
            if self_too:
                greet(d)

    xs[...] = jnp.concatenate(
        [xin[...].astype(F32), jnp.zeros((PAD - HALF, 8 * PW), F32)], axis=0
    ).astype(BF16)
    pl.semaphore_wait(barrier, 21 + 2 * other)

    for device, cc, zz, self_too in way_in:
        move(
            xs.at[:, cols_at((cc * 4 + zz) * PW, PW)],
            ain.at[rows_at((z * 2 + k) * PAD, PAD)],
            sem_send.at[0, 1 if self_too else 0],
            sem_a2a.at[z * 2 + k],
            device,
            self_too,
        )

    my_slot = (r_x * 2 + k) * 4 + y
    my_rows = rows_at(my_slot * ROWS, ROWS)

    def assemble(u):
        parts = []
        for kk in range(2):
            ref = ain.at[pl.ds((u * 2 + kk) * PAD, PAD)]
            wait_bytes(ref, sem_a2a.at[u * 2 + kk])
            parts.append(ref[...].astype(F32)[:HALF])
        xp[u, my_rows, :] = jnp.concatenate(parts, axis=0).astype(BF16)

    class Gather:
        IDX = {
            (0, -1, "AB"): 0,
            (0, 1, "AB"): 1,
            (0, 2, "AB"): 2,
            (1, 0, "AB"): 3,
            (1, -1, "A"): 4,
            (1, -1, "B"): 5,
            (1, 1, "A"): 6,
            (1, 1, "B"): 7,
            (1, 2, "A"): 8,
            (1, 2, "B"): 9,
        }

        def __init__(self, buf, i, par, u, cols):
            self.buf, self.i, self.u = buf, i, u
            self.par = par
            self.start, self.width, self.cut = cols

        def area(self, rows):
            return self.buf.at[self.u, rows, pl.ds(self.start, self.width)]

        def piece(self, s, e, part="AB"):
            rr = r_x if s == 0 else 1 - r_x
            slot = (rr * 2 + k) * 4 + (y + e + 4) % 4
            cols = pl.ds(self.start, self.width)
            if part == "A":
                cols = pl.ds(self.start, self.cut)
            elif part == "B":
                cols = pl.ds(self.start + self.cut, self.width - self.cut)
            return self.buf.at[self.u, rows_at(slot * ROWS, ROWS), cols]

        def rsem(self, *key):
            return sem_ag.at[self.i, self.IDX[key]]

        def send(self, s, e, part, device, key):
            ref = self.piece(s, e, part)
            rdma(ref, ref, sem_agd.at[self.i, 0], self.rsem(*key), device).start()

        def side(self, s, kk):
            rr = r_x if s == 0 else 1 - r_x
            return self.area(rows_at((rr * 2 + kk) * SIDE, SIDE))

        def to_sib(self, s):
            ref = self.side(s, k)
            rdma(
                ref, ref, sem_agd.at[self.i, 1], sem_agd.at[self.i, 2 + s], sib
            ).start()

        def wait(self, s, e, part):
            wait_bytes(self.piece(s, e, part), self.rsem(s, e, part))

        def o(self):
            self.send(0, 0, "AB", ring[1], (0, -1, "AB"))
            self.send(0, 0, "AB", ring[-1], (0, 1, "AB"))
            self.send(0, 0, "AB", pair, (1, 0, "AB"))

        def p(self):
            self.wait(1, 0, "AB")
            for s in (self.par, -self.par):
                self.send(1, 0, "B", ring[s], (1, -s, "B"))

        def first(self, e):
            self.wait(0, e, "AB")
            if e == -self.par:
                self.send(0, e, "AB", ring[self.par], (0, 2, "AB"))
            self.send(0, e, "A", pair, (1, e, "A"))

        def m(self):
            self.first(-1)

        def q(self):
            self.first(1)

        def b(self):
            self.wait(1, -self.par, "B")
            self.send(1, -self.par, "B", ring[self.par], (1, 2, "B"))

        def r(self):
            self.wait(0, 2, "AB")
            self.send(0, 2, "A", pair, (1, 2, "A"))
            self.to_sib(0)

        def e(self):
            self.wait(1, self.par, "B")
            for e in (-1, 1):
                self.wait(1, e, "A")
            self.wait(1, 2, "B")
            self.wait(1, 2, "A")
            self.to_sib(1)

        def here(self, s):
            wait_bytes(self.side(s, 1 - k), sem_agd.at[self.i, 2 + s])

        def sent(self):
            wait_bytes(self.area(pl.ds(0, 7 * ROWS)), sem_agd.at[self.i, 0])
            wait_bytes(self.area(pl.ds(0, 2 * SIDE)), sem_agd.at[self.i, 1])

    ax = [Gather(xp, u, 1 - 2 * (u % 2), u, X_PASS) for u in range(4)]
    steps = [z, (z + 3) % 4, (z + 1) % 4, (z + 2) % 4]
    ay = [
        [
            Gather(yp, 4 + 4 * n + t, 1 - 2 * (t % 2), steps[t], cols)
            for t in range(4)
        ]
        for n, cols in enumerate(Y_PASS)
    ]

    def side_start(c):
        return (r_x if c == 0 else 1 - r_x) * HB

    def side_cols(c):
        return cols_at(side_start(c), HB)

    def partial_gram(u, c):
        ax[u].here(c)
        tile = jnp.concatenate([xp[v, my_rows, :] for v in range(4)], axis=0)
        for start, n in ((0, 512), (512, 384)):
            part = lax.dot_general(
                tile,
                xp[u, rows_at(side_start(c) + start, n), :],
                (((1,), (1,)), ((), ())),
                preferred_element_type=F32,
            ).astype(BF16)
            cols = cols_at(side_start(c) + start, n)
            for v in range(4):
                pbuf[u, v, :, cols] = part[v * ROWS : (v + 1) * ROWS]
        s = 1 if c == 0 else -1
        h = side_cols(c)
        rs_send(pbuf.at[u, (z + 2) % 4, :, h], rbuf.at[u, 0, :, h], u, c, 0, zring[s])
        rs_send(
            pbuf.at[u, (z + 4 - s) % 4, :, h], rbuf.at[u, 1, :, h], u, c, 1, zring[-s]
        )

    def rs_send(src, dst, u, c, i, device):
        rdma(src, dst, sem_send.at[1, u], sem_rs.at[u * 2 + c, i], device).start()

    def rs_mid(u, c):
        s = 1 if c == 0 else -1
        h = side_cols(c)
        v = (z + 4 + s) % 4
        wait_bytes(rbuf.at[u, 0, :, h], sem_rs.at[u * 2 + c, 0])
        pbuf[u, v, :, h] = (
            pbuf[u, v, :, h].astype(F32) + rbuf[u, 0, :, h].astype(F32)
        ).astype(BF16)
        rs_send(pbuf.at[u, v, :, h], rbuf.at[u, 2, :, h], u, c, 2, zring[s])

    def rs_sum(u, c):
        h = side_cols(c)
        wait_bytes(rbuf.at[u, 1, :, h], sem_rs.at[u * 2 + c, 1])
        wait_bytes(rbuf.at[u, 2, :, h], sem_rs.at[u * 2 + c, 2])
        pbuf[u, z, :, h] = (
            pbuf[u, z, :, h].astype(F32)
            + rbuf[u, 1, :, h].astype(F32)
            + rbuf[u, 2, :, h].astype(F32)
        ).astype(BF16)
        rs_send(pbuf.at[u, z, :, h], rx.at[u, :, h], u, c, 3, cpair)

    def rs_end(u, c):
        h = side_cols(c)
        wait_bytes(rx.at[u, :, h], sem_rs.at[u * 2 + c, 3])
        total = pbuf[u, z, :, h].astype(F32) + rx[u, :, h].astype(F32)
        gb[z, u, :, h] = (total * inv_square).astype(BF16)

    def g_u(j):
        return c_x if j == 0 else j

    def gref(e, u, half=None):
        ref = gb.at[(z + e + 4) % 4, u]
        return ref if half is None else ref.at[:, pl.ds(half * HB, HB)]

    def g_send(ref, device, i):
        rdma(ref, ref, sem_send.at[2, 0], sem_g.at[i], device).start()

    def g_own(j):
        g_send(gref(0, g_u(j)), zring[1], 4 * j)
        g_send(gref(0, g_u(j)), zring[-1], 4 * j + 1)

    def g_pass(j, e):
        u = g_u(j)
        wait_bytes(gref(e, u), sem_g.at[4 * j + (0 if e == -1 else 1)])
        half = 0 if e == -1 else 1
        g_send(gref(e, u, half), zring[-e], 4 * j + 2 + half)
        if j == 0:
            g_send(gref(e, u), cpair, 16 + half)

    def g_far(j):
        for half in range(2):
            wait_bytes(gref(2, g_u(j), half), sem_g.at[4 * j + 2 + half])

    def g_far_pair():
        g_far(0)
        g_send(gref(2, g_u(0)), cpair, 18)

    def g_pair(e):
        wait_bytes(gref(e, 1 - c_x), sem_g.at[16 + (-1, 1, 2).index(e)])

    def first_prod(t):
        if t > 0:
            g_pair((0, -1, 1, 2)[t])
        if t == 3:
            g_far(2)
            g_far(3)
        v = steps[t]
        acc = zacc.at[pl.ds(0, ROWS)]
        acc[...] = jnp.dot(gb[v, 0], xp[0], preferred_element_type=F32)
        for u in range(1, 3):
            acc[...] += jnp.dot(gb[v, u], xp[u], preferred_element_type=F32)
        yp[v, my_rows, :] = (
            acc[...] + jnp.dot(gb[v, 3], xp[3], preferred_element_type=F32)
        ).astype(BF16)

    def second_prod(n, t):
        ay[n][t].here(0)
        ay[n][t].here(1)
        v = steps[t]
        cols = pl.ds(Y_PASS[n][0], Y_PASS[n][1])
        g = jnp.concatenate([gb[i, v] for i in range(4)], axis=0)
        term = jnp.dot(g, yp[v, :, cols], preferred_element_type=F32)
        if t == 0:
            zacc[:, cols] = term
        else:
            zacc[:, cols] += term

    def combine(n):
        cols = pl.ds(Y_PASS[n][0], Y_PASS[n][1])
        gap = jnp.zeros((PAD - HALF, Y_PASS[n][1]), F32)
        for v in range(4):
            it = (
                coef_a * xp[v, my_rows, cols].astype(F32)
                + coef_b * yp[v, my_rows, cols].astype(F32)
                + coef_c * zacc[pl.ds(v * ROWS, ROWS), cols]
            )
            for kk in range(2):
                fin[pl.ds((v * 2 + kk) * PAD, PAD), cols] = jnp.concatenate(
                    [it[kk * HALF : (kk + 1) * HALF], gap], axis=0
                ).astype(BF16)
        for device, zz, kk, self_too in way_back:
            move(
                fin.at[rows_at((zz * 2 + kk) * PAD, PAD), cols],
                oin.at[rows_at((c_x * 4 + z) * PAD, PAD), cols],
                sem_send.at[3 + n, 1 if self_too else 0],
                sem_back.at[n, c_x * 4 + z],
                device,
                self_too,
            )

    def collect(n):
        start, width, _ = Y_PASS[n]
        for g in range(8):
            ref = oin.at[pl.ds(g * PAD, PAD), pl.ds(start, width)]
            wait_bytes(ref, sem_back.at[n, g])
            out[:, pl.ds(g * PW + start, width)] = (
                ref[...].astype(F32)[:HALF].astype(BF16)
            )

    for name in ORDER:
        kind, args = name[0], [int(i) for i in name[1:] if i.isdigit()]
        if kind == "x":
            getattr(ax[args[0]], name[-1])()
        elif kind == "y":
            getattr(ay[args[0]][args[1]], name[-1])()
        elif kind in "ij":
            g_pass(args[0], -1 if kind == "i" else 1)
        else:
            {
                "a": assemble,
                "g": partial_gram,
                "s": rs_mid,
                "t": rs_sum,
                "w": rs_end,
                "h": g_own,
                "k": lambda _: g_far_pair(),
                "f": first_prod,
                "z": second_prod,
                "o": combine,
                "v": collect,
            }[kind](*args)

    for g in (*ax, *(g for n in ay for g in n)):
        g.sent()
    for u in range(4):
        wait_bytes(pbuf.at[u], sem_send.at[1, u])
    wait_bytes(gb.at[pl.ds(0, 3)], sem_send.at[2, 0])
    wait_bytes(ain.at[pl.ds(0, 7 * PAD)], sem_send.at[0, 0])
    for n, (start, width, _) in enumerate(Y_PASS):
        wait_bytes(
            fin.at[pl.ds(0, 7 * PAD), pl.ds(start, width)], sem_send.at[3 + n, 0]
        )

    @pl.when(jnp.logical_not(same))
    def _():
        wait_bytes(ain.at[pl.ds(0, PAD)], sem_send.at[0, 1])
        for n, (start, width, _) in enumerate(Y_PASS):
            wait_bytes(
                fin.at[pl.ds(0, PAD), pl.ds(start, width)], sem_send.at[3 + n, 1]
            )


def solution(mesh):
    def step(ortho_in):
        rows, full_cols = ortho_in.shape
        full_rows = rows * mesh.size
        inv_square = 1.0 / (math.sqrt(full_rows) + math.sqrt(full_cols)) ** 2
        vmem = pltpu.VMEM
        dma = pltpu.SemaphoreType.DMA
        n = len(Y_PASS)
        return pl.pallas_call(
            functools.partial(kernel, inv_square),
            name="newton_schulz",
            out_shape=jax.ShapeDtypeStruct((rows, full_cols), BF16),
            in_specs=[pl.BlockSpec(memory_space=pltpu.VMEM)],
            out_specs=pl.BlockSpec(memory_space=pltpu.VMEM),
            scratch_shapes=[
                vmem((PAD, 8 * PW), BF16),
                vmem((8 * PAD, PW), BF16),
                vmem((4, BLK, PW), BF16),
                vmem((4, BLK, PW), BF16),
                vmem((4, 4, ROWS, BLK), BF16),
                vmem((4, 3, ROWS, BLK), BF16),
                vmem((4, ROWS, BLK), BF16),
                vmem((4, 4, ROWS, BLK), BF16),
                vmem((4 * ROWS, PW), F32),
                vmem((8 * PAD, PW), BF16),
                vmem((8 * PAD, PW), BF16),
                dma((8,)),
                dma((4 + 4 * n, 10)),
                dma((4 + 4 * n, 4)),
                dma((8, 4)),
                dma((19,)),
                dma((n, 8)),
                dma((3 + n, 4)),
            ],
            compiler_params=pltpu.CompilerParams(
                collective_id=0,
                has_side_effects=True,
                vmem_limit_bytes=64 * 2**20 - 2**18,
            ),
            cost_estimate=pl.CostEstimate(
                flops=3 * 2 * 448 * 7168 * 1152,
                bytes_accessed=4 * 56 * 9216,
                transcendentals=0,
            ),
        )(ortho_in)

    spec = P(("row", "col"), None)
    return jax.shard_map(
        step, mesh=mesh, in_specs=(spec,), out_specs=spec, check_vma=False
    )
```

time: 554 us -> 201 us (0.36)
  waiting for transfers between devices: 449 us -> 0 us
  Pallas kernels: 0 us -> 198 us
  blocking collectives: 47 us -> 0 us
  matrix products: 41.7 us -> 0 us
  between operations: 13.1 us -> 0.01 us
    psum x1 -> x0, waiting for transfers between devices: 269 us -> none  [per_device(): lax.psum(partial_gram.astype(jnp.bfloat16), 'col').astype(jnp.float32)]
    pallas_call x0 -> x1, Pallas kernels: none -> 198 us  [step(): pl.pallas_call(functools.partial(kernel, inv_square), name='newton_schulz...]
    all_gather x2 -> x0, waiting for transfers between devices: 180 us -> none  [the longest x1 90.8 us: per_device(): lax.all_gather(first_prod, 'row', axis=0, tiled=True)]
    all_to_all x2 -> x0, blocking collectives: 47 us -> none  [the longest x1 24.3 us: per_device(): lax.all_to_all(ortho_in, 'col', split_axis=1, concat_axis=0, tiled=True)]
    dot_general x3 -> x0, matrix products: 41.7 us -> none  [the longest x1 14 us: per_device(): first_f = jnp.dot(gram, panel, preferred_element_type=jnp.float32)]
  transfers between devices with their start and end apart: 3 -> 0, of which waited for: 3 -> 0; matrix products, arithmetic and copies ran while one was open for 0% -> 0% of each run, Pallas kernels for 0% -> 0%
where the time goes in v2:
time: 201 us; the launch traced here: 200 us
  Pallas kernels  198 us (99%)
  local copies, waits for them, and re-layouts  2.25 us (1%)
    pallas_call x1, Pallas kernels, step(): pl.pallas_call(functools.partial(kernel, inv_square), name='newton_schulz...  198 us

profile of v2, /device:TPU:1, one launch (start us, length us, event | category | flops | bytes accessed | tf_op | source)
XLA Modules:
  0.0 199.9 jit_solution(3941745852783115632)
XLA Ops:
  0.0 197.6 %newton_schulz.1 = bf16[56,9216]{1,0:T(8,128)(2,1)} custom-call(bf16[56,9216]{1,0:T(8,128)(2,1)} %xin.1), custom_call_target="tpu_custom_call" | custom-call | flops 22196256768 | bytes 2064384 | tf_op jit(solution)/shard_map/newton_schulz/pallas_call | solution.py:484
  197.6 2.2 %copy.3 = bf16[56,9216]{1,0:T(8,128)(2,1)} copy(bf16[56,9216]{1,0:T(8,128)(2,1)} %newton_schulz.1) | data formatting | bytes 2064384

commit v3 on v2

--- a/solution.py
+++ b/solution.py
@@ -27,18 +27,20 @@
 Y_PASS = ((0, 640, 256), (640, 512, 256))
 
 ORDER = (
-    "a0", "x0o", "a1", "x1o", "a2", "a3", "x0m", "x0q", "x0p", "x1m", "x1q", "x1p", "x0r", "x0b",
-    "x1r", "x2o", "g00", "x1b", "g10", "x0e", "s00", "x2q", "g01", "x2m", "x1e", "x3o", "s10",
-    "x2p", "g11", "t00", "s01", "x2r", "x3q", "x3p", "g20", "w00", "s11", "x3m", "t10", "t01",
-    "x2b", "x3r", "x3b", "g30", "w10", "x2e", "s20", "t11", "w01", "x3e", "g21", "s30", "g31",
-    "w11", "t20", "s21", "s31", "w20", "t30", "t21", "t31", "h0", "w30", "w21", "h2", "w31", "h3",
-    "f0", "i0", "j0", "y10o", "y00o", "y10m", "y10p", "y10q", "i2", "j2", "y00m", "y00q", "y00p",
-    "y10r", "y10b", "y00r", "i3", "j3", "f1", "y00b", "y11o", "y10e", "y01o", "f2", "k0", "y00e",
-    "y12o", "y11p", "y11q", "y02o", "y11m", "y01q", "y01p", "y01m", "y12q", "y12p", "y11b", "y12m",
-    "y11r", "f3", "z10", "z00", "y01r", "y12b", "y02q", "y02m", "y02p", "y13o", "y12r", "y01b",
-    "y03o", "y11e", "y02r", "z11", "y13p", "y02b", "y13q", "y12e", "y01e", "y13m", "z12", "z01",
-    "y13b", "y03q", "y03m", "y03p", "y02e", "y13r", "z02", "y13e", "y03r", "y03b", "z13", "o1",
-    "y03e", "z03", "o0", "v1", "v0",
+    "a0", "x0o", "a1", "x1o", "a2", "a3", "x0m", "x0q", "x0p", "x1m", "x1q", "x1p", "x2o", "x0r",
+    "x0b", "x1r", "g00", "g01", "x1b", "g10", "g11", "s00", "x2p", "s01", "x2m", "x2q", "x3o",
+    "s10", "x0e", "x1e", "s11", "t01", "t00", "x2b", "g02", "g03", "t11", "t10", "g12", "w01",
+    "g13", "w00", "s02", "x2r", "x3q", "w11", "s03", "x3p", "g20", "s12", "w10", "g21", "x3m",
+    "s13", "x3r", "t03", "t02", "x2e", "s20", "x3b", "g30", "w03", "g31", "g22", "t12", "t13",
+    "w02", "g23", "s21", "x3e", "t20", "w12", "s30", "g32", "s31", "w13", "g33", "s22", "w20",
+    "s23", "t21", "t30", "s32", "w21", "t31", "s33", "w30", "t23", "w31", "h0", "t22", "t33", "t32",
+    "w23", "w22", "h2", "w33", "w32", "h3", "i0", "f0", "j0", "y00o", "y10o", "y00m", "i2", "y00p",
+    "y00q", "j2", "y10m", "y10q", "y10p", "y00r", "y00b", "i3", "f1", "j3", "y01o", "y10b", "y10r",
+    "y11o", "y00e", "f2", "k0", "y02o", "y12o", "y01m", "y01q", "y01p", "y10e", "y11q", "y11m",
+    "y11p", "y02q", "y02m", "y02p", "y12q", "y12m", "y12p", "f3", "y01r", "z10", "y01b", "y13o",
+    "z00", "y11r", "y02r", "y11b", "y03o", "y02b", "y12r", "y12b", "y01e", "y13p", "y13m", "y13q",
+    "z01", "y11e", "y03m", "y02e", "y03p", "z11", "y12e", "y13b", "y03q", "z02", "y13r", "z12",
+    "y03b", "y13e", "y03r", "z13", "o1", "y03e", "z03", "o0", "v1", "v0",
 )
 
 
@@ -46,6 +48,7 @@
     inv_square,
     xin,
     out,
+    xv,
     xs,
     ain,
     xp,
@@ -56,7 +59,7 @@
     gb,
     zacc,
     fin,
-    oin,
+    sem_in,
     sem_a2a,
     sem_ag,
     sem_agd,
@@ -119,6 +122,9 @@
         def _():
             rdma(src, dst, ssem, rsem, device).start()
 
+    load = pltpu.make_async_copy(xin, xv, sem_in.at[0])
+    load.start()
+
     barrier = pltpu.get_barrier_semaphore()
 
     def greet(device):
@@ -136,22 +142,22 @@
             kk = k if i == 0 else 1 - k
             zz = (z + d) % 4
             way_back.append((dev(x_far, y, zz, kk), zz, kk, d == 0 and i == 0))
-    for d in (ring[1], ring[-1], pair, zring[1], zring[-1], cpair, sib):
+    for d in (ring[1], ring[-1], pair, sib):
         greet(d)
-    for d, _, _, self_too in way_in + way_back:
+    for d, _, _, self_too in way_back:
         if not self_too:
             greet(d)
+    back_self = way_back[-2][0]
 
     @pl.when(jnp.logical_not(same))
     def _():
-        for d, _, _, self_too in way_in + way_back:
-            if self_too:
-                greet(d)
-
+        greet(back_self)
+
+    load.wait()
     xs[...] = jnp.concatenate(
-        [xin[...].astype(F32), jnp.zeros((PAD - HALF, 8 * PW), F32)], axis=0
+        [xv[...].astype(F32), jnp.zeros((PAD - HALF, 8 * PW), F32)], axis=0
     ).astype(BF16)
-    pl.semaphore_wait(barrier, 21 + 2 * other)
+    pl.semaphore_wait(barrier, 11 + other)
 
     for device, cc, zz, self_too in way_in:
         move(
@@ -285,46 +291,48 @@
     def side_start(c):
         return (r_x if c == 0 else 1 - r_x) * HB
 
-    def side_cols(c):
-        return cols_at(side_start(c), HB)
+    UNITS = ((0, 0, 512, 1), (0, 512, 384, -1), (1, 0, 512, -1), (1, 512, 384, 1))
+
+    def unit_cols(c):
+        side, start, n, _ = UNITS[c]
+        return cols_at(side_start(side) + start, n)
 
     def partial_gram(u, c):
-        ax[u].here(c)
+        side, start, n, s = UNITS[c]
+        if start == 0:
+            ax[u].here(side)
         tile = jnp.concatenate([xp[v, my_rows, :] for v in range(4)], axis=0)
-        for start, n in ((0, 512), (512, 384)):
-            part = lax.dot_general(
-                tile,
-                xp[u, rows_at(side_start(c) + start, n), :],
-                (((1,), (1,)), ((), ())),
-                preferred_element_type=F32,
-            ).astype(BF16)
-            cols = cols_at(side_start(c) + start, n)
-            for v in range(4):
-                pbuf[u, v, :, cols] = part[v * ROWS : (v + 1) * ROWS]
-        s = 1 if c == 0 else -1
-        h = side_cols(c)
+        part = lax.dot_general(
+            tile,
+            xp[u, rows_at(side_start(side) + start, n), :],
+            (((1,), (1,)), ((), ())),
+            preferred_element_type=F32,
+        ).astype(BF16)
+        h = unit_cols(c)
+        for v in range(4):
+            pbuf[u, v, :, h] = part[v * ROWS : (v + 1) * ROWS]
         rs_send(pbuf.at[u, (z + 2) % 4, :, h], rbuf.at[u, 0, :, h], u, c, 0, zring[s])
         rs_send(
             pbuf.at[u, (z + 4 - s) % 4, :, h], rbuf.at[u, 1, :, h], u, c, 1, zring[-s]
         )
 
     def rs_send(src, dst, u, c, i, device):
-        rdma(src, dst, sem_send.at[1, u], sem_rs.at[u * 2 + c, i], device).start()
+        rdma(src, dst, sem_send.at[1, u], sem_rs.at[u * 4 + c, i], device).start()
 
     def rs_mid(u, c):
-        s = 1 if c == 0 else -1
-        h = side_cols(c)
+        s = UNITS[c][3]
+        h = unit_cols(c)
         v = (z + 4 + s) % 4
-        wait_bytes(rbuf.at[u, 0, :, h], sem_rs.at[u * 2 + c, 0])
+        wait_bytes(rbuf.at[u, 0, :, h], sem_rs.at[u * 4 + c, 0])
         pbuf[u, v, :, h] = (
             pbuf[u, v, :, h].astype(F32) + rbuf[u, 0, :, h].astype(F32)
         ).astype(BF16)
         rs_send(pbuf.at[u, v, :, h], rbuf.at[u, 2, :, h], u, c, 2, zring[s])
 
     def rs_sum(u, c):
-        h = side_cols(c)
-        wait_bytes(rbuf.at[u, 1, :, h], sem_rs.at[u * 2 + c, 1])
-        wait_bytes(rbuf.at[u, 2, :, h], sem_rs.at[u * 2 + c, 2])
+        h = unit_cols(c)
+        wait_bytes(rbuf.at[u, 1, :, h], sem_rs.at[u * 4 + c, 1])
+        wait_bytes(rbuf.at[u, 2, :, h], sem_rs.at[u * 4 + c, 2])
         pbuf[u, z, :, h] = (
             pbuf[u, z, :, h].astype(F32)
             + rbuf[u, 1, :, h].astype(F32)
@@ -333,8 +341,8 @@
         rs_send(pbuf.at[u, z, :, h], rx.at[u, :, h], u, c, 3, cpair)
 
     def rs_end(u, c):
-        h = side_cols(c)
-        wait_bytes(rx.at[u, :, h], sem_rs.at[u * 2 + c, 3])
+        h = unit_cols(c)
+        wait_bytes(rx.at[u, :, h], sem_rs.at[u * 4 + c, 3])
         total = pbuf[u, z, :, h].astype(F32) + rx[u, :, h].astype(F32)
         gb[z, u, :, h] = (total * inv_square).astype(BF16)
 
@@ -414,7 +422,7 @@
         for device, zz, kk, self_too in way_back:
             move(
                 fin.at[rows_at((zz * 2 + kk) * PAD, PAD), cols],
-                oin.at[rows_at((c_x * 4 + z) * PAD, PAD), cols],
+                out.at[rows_at((c_x * 4 + z) * PAD, PAD), cols],
                 sem_send.at[3 + n, 1 if self_too else 0],
                 sem_back.at[n, c_x * 4 + z],
                 device,
@@ -424,11 +432,8 @@
     def collect(n):
         start, width, _ = Y_PASS[n]
         for g in range(8):
-            ref = oin.at[pl.ds(g * PAD, PAD), pl.ds(start, width)]
+            ref = fin.at[pl.ds(g * PAD, PAD), pl.ds(start, width)]
             wait_bytes(ref, sem_back.at[n, g])
-            out[:, pl.ds(g * PW + start, width)] = (
-                ref[...].astype(F32)[:HALF].astype(BF16)
-            )
 
     for name in ORDER:
         kind, args = name[0], [int(i) for i in name[1:] if i.isdigit()]
@@ -481,13 +486,14 @@
         vmem = pltpu.VMEM
         dma = pltpu.SemaphoreType.DMA
         n = len(Y_PASS)
-        return pl.pallas_call(
+        parts = pl.pallas_call(
             functools.partial(kernel, inv_square),
             name="newton_schulz",
-            out_shape=jax.ShapeDtypeStruct((rows, full_cols), BF16),
-            in_specs=[pl.BlockSpec(memory_space=pltpu.VMEM)],
-            out_specs=pl.BlockSpec(memory_space=pltpu.VMEM),
+            out_shape=jax.ShapeDtypeStruct((8 * PAD, PW), BF16),
+            in_specs=[pl.BlockSpec(memory_space=pl.ANY)],
+            out_specs=pl.BlockSpec(memory_space=pl.ANY),
             scratch_shapes=[
+                vmem((HALF, 8 * PW), BF16),
                 vmem((PAD, 8 * PW), BF16),
                 vmem((8 * PAD, PW), BF16),
                 vmem((4, BLK, PW), BF16),
@@ -498,11 +504,11 @@
                 vmem((4, 4, ROWS, BLK), BF16),
                 vmem((4 * ROWS, PW), F32),
                 vmem((8 * PAD, PW), BF16),
-                vmem((8 * PAD, PW), BF16),
+                dma((1,)),
                 dma((8,)),
                 dma((4 + 4 * n, 10)),
                 dma((4 + 4 * n, 4)),
-                dma((8, 4)),
+                dma((16, 4)),
                 dma((19,)),
                 dma((n, 8)),
                 dma((3 + n, 4)),
@@ -518,6 +524,8 @@
                 transcendentals=0,
             ),
         )(ortho_in)
+        parts = parts.reshape(8, PAD, PW)[:, :HALF]
+        return parts.transpose(1, 0, 2).reshape(rows, full_cols)
 
     spec = P(("row", "col"), None)
     return jax.shard_map(

time: 201 us -> 195 us (0.970)
  Pallas kernels: 198 us -> 192 us
    pallas_call x1, Pallas kernels: 198 us -> 192 us  [step(): pl.pallas_call(functools.partial(kernel, inv_square), name='newton_schulz...]
where the time goes in v3:
time: 195 us; the launch traced here: 194 us
  Pallas kernels  192 us (98%)
  local copies, waits for them, and re-layouts  2.39 us (1%)
    pallas_call x1, Pallas kernels, step(): pl.pallas_call(functools.partial(kernel, inv_square), name='newton_schulz...  192 us

profile of v3, /device:TPU:1, one launch (start us, length us, event | category | flops | bytes accessed | tf_op | source)
XLA Modules:
  0.0 194.4 jit_solution(3028509286397829321)
XLA Ops:
  0.0 192.0 %newton_schulz.1 = bf16[512,1152]{1,0:T(8,128)(2,1)} custom-call(bf16[56,9216]{1,0:T(8,128)(2,1)} %xin.1), custom_call_target="tpu_custom_call" | custom-call | flops 22196256768 | bytes 2064384 | tf_op jit(solution)/shard_map/newton_schulz/pallas_call | solution.py:489
  192.0 1.3 slice_bitcast_fusion
  193.3 1.1 copy.3

commit v4 on v3

v4 whole, which is shorter than its diff:
```python
import functools
import math

import jax
import jax.numpy as jnp
from jax import lax
from jax.experimental import pallas as pl
from jax.experimental.pallas import tpu as pltpu
from jax.sharding import PartitionSpec as P

coef_a = 3.4445
coef_b = -4.775
coef_c = 2.0315

MESH = pl.DeviceIdType.MESH
F32 = jnp.float32
BF16 = jnp.bfloat16

STEPS = 7
T16 = 16
ROWS = STEPS * T16
HALF = 56
PAD = 64
PW = 1152
SEG = 256
BLK = 4 * SEG
UNIT = BLK // 2
X_PASS = (0, PW, 512)
Y_PASS = ((0, 512, 256), (512, 384, 128), (896, 256, 128))
RELAYED = (0, 2)

ORDER = (
    "a0", "a1", "x0o", "x1o", "a2", "a3", "x0m", "x0q", "x0p", "a4", "a5", "x1m", "x1q", "x1p",
    "a6", "x0r", "x2o", "x0b", "x1r", "g00", "x1b", "x3o", "g10", "x2m", "x2q", "x2p", "s00", "x0e",
    "x1e", "s10", "g01", "x3q", "g11", "t00", "x3p", "x3m", "x2r", "x4o", "t10", "s01", "x2b",
    "x3r", "g20", "w00", "x5o", "s11", "x3b", "g30", "w10", "t01", "x4m", "x4p", "x4q", "s20",
    "x2e", "s30", "x5q", "w01", "g21", "t11", "x3e", "t20", "x5p", "x5m", "x6o", "x4r", "g31",
    "t30", "s21", "x4b", "w11", "x5r", "g40", "x5b", "w20", "g50", "s31", "x6p", "x6m", "w30",
    "x6q", "t21", "s40", "x4e", "x5e", "x6b", "s50", "g41", "g51", "w21", "t40", "x6r", "t31",
    "t50", "g60", "x6e", "s41", "w40", "g61", "w31", "s51", "s60", "w50", "t41", "s61", "h2", "t60",
    "w41", "h4", "t51", "t61", "w60", "h0", "i2", "w51", "h5", "j2", "w61", "h6", "f0", "y00o",
    "i4", "j4", "i0", "y00m", "y00q", "y00p", "y10o", "j0", "y00r", "y10q", "y00b", "y10p", "i5",
    "j5", "y10m", "y20o", "y00e", "k2", "y10b", "y20q", "y20p", "i6", "f1", "y01o", "y11o", "j6",
    "f2", "y02o", "y10r", "y21o", "y01q", "k0", "y01p", "y01m", "y20m", "y20b", "y11m", "y11q",
    "y11p", "y02m", "y02p", "y02q", "y10e", "y21m", "y21q", "y21p", "f3", "y03o", "z00", "y01r",
    "y01b", "y11b", "y02r", "y11r", "z10", "y02b", "y12o", "y20r", "y21r", "y21b", "y03m", "y03p",
    "y03q", "y13o", "y01e", "y02e", "y12m", "y11e", "z01", "y12p", "y12q", "z02", "y03b", "y12r",
    "y20e", "y13m", "z11", "y12b", "y03r", "y22o", "y13p", "z20", "y21e", "y13q", "y23o", "y12e",
    "z21", "y03e", "y22m", "z12", "y22p", "y22q", "y13b", "z03", "o0", "y13r", "y22r", "y23p",
    "y23q", "y22b", "y23m", "y13e", "y23b", "y22e", "y23r", "z13", "o1", "z22", "y23e", "v0", "z23",
    "o2", "v1", "v2",
)


def kernel(
    inv_square,
    xin,
    out,
    xv,
    xl,
    ain,
    xp,
    yp,
    pbuf,
    rbuf,
    rx,
    gb,
    zacc,
    fin,
    sem_in,
    sem_a2a,
    sem_ag,
    sem_agd,
    sem_rs,
    sem_g,
    sem_back,
    sem_send,
):
    row, col = lax.axis_index("row"), lax.axis_index("col")
    k = row % 2
    y = (row // 2) % 4
    x = (col % 2) * 2 + row // 8
    z = col // 2
    r_x = ((x + 1) // 2) % 2
    c_x = x // 2

    def dev(xx, yy, zz, kk):
        return (((xx % 2) * 4 + yy) * 2 + kk, zz * 2 + xx // 2)

    x_row = x + 1 - 2 * (x % 2)
    x_col = 3 - x
    ring = {1: dev(x, (y + 1) % 4, z, k), -1: dev(x, (y + 3) % 4, z, k)}
    pair = dev(x_row, y, z, k)
    zring = {1: dev(x, y, (z + 1) % 4, k), -1: dev(x, y, (z + 3) % 4, k)}
    cpair = dev(x_col, y, z, k)
    sib = dev(x, y, z, 1 - k)
    same = k == c_x
    other = k + c_x - 2 * k * c_x
    x_far = x + (x_col - x) * other

    def rdma(src, dst, ssem, rsem, device):
        return pltpu.make_async_remote_copy(
            src_ref=src,
            dst_ref=dst,
            send_sem=ssem,
            recv_sem=rsem,
            device_id=device,
            device_id_type=MESH,
        )

    def wait_bytes(ref, sem):
        pltpu.make_async_copy(ref, ref, sem).wait()

    def rows_at(start, n):
        return pl.ds(pl.multiple_of(start, 16), n)

    def cols_at(start, n):
        return pl.ds(pl.multiple_of(start, 128), n)

    def move(src, dst, ssem, rsem, device, self_too):
        if not self_too:
            rdma(src, dst, ssem, rsem, device).start()
            return

        @pl.when(same)
        def _():
            pltpu.make_async_copy(src, dst, rsem).start()

        @pl.when(jnp.logical_not(same))
        def _():
            rdma(src, dst, ssem, rsem, device).start()

    load = pltpu.make_async_copy(xin, xv, sem_in.at[0])
    load.start()

    barrier = pltpu.get_barrier_semaphore()

    def greet(device):
        pl.semaphore_signal(barrier, inc=1, device_id=device, device_id_type=MESH)

    way_in = []
    for d in (0, 1, 3, 2):
        for i in range(2):
            xx, cc = (x, c_x) if i == 0 else (x_col, 1 - c_x)
            zz = (z + d) % 4
            way_in.append((dev(xx, y, zz, c_x), cc, zz, d == 0 and i == 0))
    way_back = []
    for d in (2, 1, 3, 0):
        for i in range(2):
            kk = k if i == 0 else 1 - k
            zz = (z + d) % 4
            way_back.append((dev(x_far, y, zz, kk), zz, kk, d == 0 and i == 0))
    for d in (ring[1], ring[-1], pair, sib):
        greet(d)
    for d, _, _, self_too in way_back:
        if not self_too:
            greet(d)
    back_self = way_back[-2][0]

    @pl.when(jnp.logical_not(same))
    def _():
        greet(back_self)

    pl.semaphore_wait(barrier, 11 + other)

    my_slot = (r_x * 2 + k) * 4 + y

    def slot_rows(slot):
        return rows_at(slot * T16, T16)

    their_slot = slot_rows((r_x * 2 + c_x) * 4 + y)

    def distribute(i):
        for device, cc, zz, self_too in way_in:
            cols = cols_at((cc * 4 + zz) * PW, PW)
            if i < 3:
                src = xin.at[pl.ds(i * T16, T16), cols]
                dst = xp.at[2 * i + k, z, their_slot]
                sem = sem_a2a.at[2 * i + k]
            else:
                src = xl.at[:, cols]
                dst = ain.at[z * 2 + k]
                sem = sem_a2a.at[6]
            move(src, dst, sem_send.at[0, 1 if self_too else 0], sem, device, self_too)

    for i in range(3):
        distribute(i)
    load.wait()
    xl[...] = jnp.concatenate(
        [xv[...].astype(F32)[48:], jnp.zeros((8, 8 * PW), F32)], axis=0
    ).astype(BF16)
    distribute(3)

    def assemble(u):
        if u < 6:
            wait_bytes(xp.at[u, :, slot_rows(my_slot)], sem_a2a.at[u])
            return
        wait_bytes(ain, sem_a2a.at[6])
        for v in range(4):
            xp[6, v, slot_rows(my_slot), :] = jnp.concatenate(
                [ain[v * 2 + kk].astype(F32)[:8] for kk in range(2)], axis=0
            ).astype(BF16)

    class Gather:
        IDX = {
            (0, -1, "AB"): 0,
            (0, 1, "AB"): 1,
            (0, 2, "AB"): 2,
            (1, 0, "AB"): 3,
            (1, -1, "A"): 4,
            (1, -1, "B"): 5,
            (1, 1, "A"): 6,
            (1, 1, "B"): 7,
            (1, 2, "A"): 8,
            (1, 2, "B"): 9,
        }

        def __init__(self, i, par, cols, area, whole):
            self.i, self.par, self.area, self.whole = i, par, area, whole
            self.start, self.width, self.cut = cols

        def piece(self, s, e, part="AB"):
            rr = r_x if s == 0 else 1 - r_x
            slot = (rr * 2 + k) * 4 + (y + e + 4) % 4
            cols = pl.ds(self.start, self.width)
            if part == "A":
                cols = pl.ds(self.start, self.cut)
            elif part == "B":
                cols = pl.ds(self.start + self.cut, self.width - self.cut)
            return self.area(slot_rows(slot), cols)

        def rsem(self, *key):
            return sem_ag.at[self.i, self.IDX[key]]

        def send(self, s, e, part, device, key):
            ref = self.piece(s, e, part)
            rdma(ref, ref, sem_agd.at[self.i, 0], self.rsem(*key), device).start()

        def side(self, s, kk):
            rr = r_x if s == 0 else 1 - r_x
            return self.area(
                rows_at((rr * 2 + kk) * 4 * T16, 4 * T16),
                pl.ds(self.start, self.width),
            )

        def to_sib(self, s):
            ref = self.side(s, k)
            rdma(
                ref, ref, sem_agd.at[self.i, 1], sem_agd.at[self.i, 2 + s], sib
            ).start()

        def wait(self, s, e, part):
            wait_bytes(self.piece(s, e, part), self.rsem(s, e, part))

        def o(self):
            self.send(0, 0, "AB", ring[1], (0, -1, "AB"))
            self.send(0, 0, "AB", ring[-1], (0, 1, "AB"))
            self.send(0, 0, "AB", pair, (1, 0, "AB"))

        def p(self):
            self.wait(1, 0, "AB")
            for s in (self.par, -self.par):
                self.send(1, 0, "B", ring[s], (1, -s, "B"))

        def first(self, e):
            self.wait(0, e, "AB")
            if e == -self.par:
                self.send(0, e, "AB", ring[self.par], (0, 2, "AB"))
            self.send(0, e, "A", pair, (1, e, "A"))

        def m(self):
            self.first(-1)

        def q(self):
            self.first(1)

        def b(self):
            self.wait(1, -self.par, "B")
            self.send(1, -self.par, "B", ring[self.par], (1, 2, "B"))

        def r(self):
            self.wait(0, 2, "AB")
            self.send(0, 2, "A", pair, (1, 2, "A"))
            self.to_sib(0)

        def e(self):
            self.wait(1, self.par, "B")
            for e in (-1, 1):
                self.wait(1, e, "A")
            self.wait(1, 2, "B")
            self.wait(1, 2, "A")
            self.to_sib(1)

        def here(self, s):
            wait_bytes(self.side(s, 1 - k), sem_agd.at[self.i, 2 + s])

        def sent(self):
            cols = pl.ds(self.start, self.width)
            wait_bytes(self.whole(cols), sem_agd.at[self.i, 0])
            wait_bytes(self.area(pl.ds(0, 8 * T16), cols), sem_agd.at[self.i, 1])

    def x_gather(u):
        return Gather(
            u,
            1 - 2 * (u % 2),
            X_PASS,
            lambda rows, cols: xp.at[u, :, rows, cols],
            lambda cols: xp.at[u, :, pl.ds(0, 7 * T16), cols],
        )

    def y_gather(n, t):
        return Gather(
            STEPS + 4 * n + t,
            1 - 2 * (t % 2),
            Y_PASS[n],
            lambda rows, cols: yp.at[:, steps[t], rows, cols],
            lambda cols: yp.at[:, 0, pl.ds(0, 7 * T16), cols],
        )

    steps = [z, (z + 3) % 4, (z + 1) % 4, (z + 2) % 4]
    ax = [x_gather(u) for u in range(STEPS)]
    ay = [[y_gather(n, t) for t in range(4)] for n in range(len(Y_PASS))]

    def side_rows(c):
        rr = r_x if c == 0 else 1 - r_x
        return rows_at(rr * 128, 128)

    def partial_gram(u, c):
        ax[u].here(c)
        tile = jnp.concatenate(
            [
                xp[i, v, slot_rows(my_slot), :]
                for v in range(4)
                for i in range(STEPS)
            ],
            axis=0,
        )
        part = lax.dot_general(
            tile,
            xp[u, :, side_rows(c), :].reshape(UNIT, PW),
            (((1,), (1,)), ((), ())),
            preferred_element_type=F32,
        ).astype(BF16)
        for v in range(4):
            pbuf[u, c, v] = part[v * ROWS : (v + 1) * ROWS]
        s = 1 if c == 0 else -1
        rs_send(pbuf.at[u, c, (z + 2) % 4], rbuf.at[u, c, 0], u, c, 0, zring[s])
        rs_send(pbuf.at[u, c, (z + 4 - s) % 4], rbuf.at[u, c, 1], u, c, 1, zring[-s])

    def rs_send(src, dst, u, c, i, device):
        rdma(src, dst, sem_send.at[1, u], sem_rs.at[u * 2 + c, i], device).start()

    def rs_mid(u, c):
        s = 1 if c == 0 else -1
        v = (z + 4 + s) % 4
        wait_bytes(rbuf.at[u, c, 0], sem_rs.at[u * 2 + c, 0])
        pbuf[u, c, v] = (
            pbuf[u, c, v].astype(F32) + rbuf[u, c, 0].astype(F32)
        ).astype(BF16)
        rs_send(pbuf.at[u, c, v], rbuf.at[u, c, 2], u, c, 2, zring[s])

    def rs_sum(u, c):
        wait_bytes(rbuf.at[u, c, 1], sem_rs.at[u * 2 + c, 1])
        wait_bytes(rbuf.at[u, c, 2], sem_rs.at[u * 2 + c, 2])
        pbuf[u, c, z] = (
            pbuf[u, c, z].astype(F32)
            + rbuf[u, c, 1].astype(F32)
            + rbuf[u, c, 2].astype(F32)
        ).astype(BF16)
        rs_send(pbuf.at[u, c, z], rx.at[u, c], u, c, 3, cpair)

    def rs_end(u, c):
        wait_bytes(rx.at[u, c], sem_rs.at[u * 2 + c, 3])
        total = pbuf[u, c, z].astype(F32) + rx[u, c].astype(F32)
        done = (total * inv_square).astype(BF16)
        rr = r_x if c == 0 else 1 - r_x
        for v in range(4):
            gb[z, u, :, cols_at(v * SEG + rr * 128, 128)] = done[
                :, v * 128 : (v + 1) * 128
            ]

    CLASSES = list(RELAYED) + [
        b for b in range(STEPS) if b not in RELAYED and b - 1 not in RELAYED
    ]

    def g_u(b):
        return b + c_x if b in RELAYED else b

    def gref(e, u, half=None):
        ref = gb.at[(z + e + 4) % 4, u]
        return ref if half is None else ref.at[:, pl.ds(half * UNIT, UNIT)]

    def g_send(ref, device, b, i):
        rdma(ref, ref, sem_send.at[2, 0], sem_g.at[b, i], device).start()

    def g_own(b):
        g_send(gref(0, g_u(b)), zring[1], b, 0)
        g_send(gref(0, g_u(b)), zring[-1], b, 1)

    def g_pass(b, e):
        u = g_u(b)
        half = 0 if e == -1 else 1
        wait_bytes(gref(e, u), sem_g.at[b, half])
        g_send(gref(e, u, half), zring[-e], b, 2 + half)
        if b in RELAYED:
            g_send(gref(e, u), cpair, b, 4 + half)

    def g_far(b):
        for half in range(2):
            wait_bytes(gref(2, g_u(b), half), sem_g.at[b, 2 + half])

    def g_far_pair(b):
        g_far(b)
        g_send(gref(2, g_u(b)), cpair, b, 6)

    def first_prod(t):
        e = (0, -1, 1, 2)[t]
        if t > 0:
            for b in RELAYED:
                wait_bytes(gref(e, b + 1 - c_x), sem_g.at[b, 3 + t])
        if t == 3:
            for b in CLASSES:
                if b not in RELAYED:
                    g_far(b)
        v = steps[t]
        acc = zacc.at[pl.ds(0, ROWS)]
        for u in range(STEPS):
            term = jnp.dot(
                gb[v, u], xp[u].reshape(BLK, PW), preferred_element_type=F32
            )
            if u == 0:
                acc[...] = term
            else:
                acc[...] += term
        for i in range(STEPS):
            yp[i, v, slot_rows(my_slot), :] = acc[pl.ds(i * T16, T16), :].astype(BF16)

    def second_prod(n, t):
        ay[n][t].here(0)
        ay[n][t].here(1)
        v = steps[t]
        cols = pl.ds(Y_PASS[n][0], Y_PASS[n][1])
        g = jnp.concatenate(
            [
                jnp.concatenate(
                    [gb[j, i, :, cols_at(v * SEG, SEG)] for i in range(STEPS)], axis=1
                )
                for j in range(4)
            ],
            axis=0,
        )
        term = jnp.dot(
            g,
            yp[:, v, :, cols].reshape(STEPS * SEG, Y_PASS[n][1]),
            preferred_element_type=F32,
        )
        if t == 0:
            zacc[:, cols] = term
        else:
            zacc[:, cols] += term

    def combine(n):
        cols = pl.ds(Y_PASS[n][0], Y_PASS[n][1])
        gap = jnp.zeros((PAD - HALF, Y_PASS[n][1]), F32)
        for v in range(4):
            it = [
                coef_a * xp[i, v, slot_rows(my_slot), cols].astype(F32)
                + coef_b * yp[i, v, slot_rows(my_slot), cols].astype(F32)
                + coef_c * zacc[pl.ds(v * ROWS + i * T16, T16), cols]
                for i in range(STEPS)
            ]
            for kk in range(2):
                mine = [it[kk], it[kk + 2], it[kk + 4], it[6][kk * 8 : kk * 8 + 8], gap]
                fin[pl.ds((v * 2 + kk) * PAD, PAD), cols] = jnp.concatenate(
                    mine, axis=0
                ).astype(BF16)
        for device, zz, kk, self_too in way_back:
            move(
                fin.at[rows_at((zz * 2 + kk) * PAD, PAD), cols],
                out.at[rows_at((c_x * 4 + z) * PAD, PAD), cols],
                sem_send.at[3 + n, 1 if self_too else 0],
                sem_back.at[n, c_x * 4 + z],
                device,
                self_too,
            )

    def collect(n):
        start, width, _ = Y_PASS[n]
        for g in range(8):
            ref = fin.at[pl.ds(g * PAD, PAD), pl.ds(start, width)]
            wait_bytes(ref, sem_back.at[n, g])

    for name in ORDER:
        kind, args = name[0], [int(i) for i in name[1:] if i.isdigit()]
        if kind == "x":
            getattr(ax[args[0]], name[-1])()
        elif kind == "y":
            getattr(ay[args[0]][args[1]], name[-1])()
        elif kind in "ij":
            g_pass(args[0], -1 if kind == "i" else 1)
        else:
            {
                "a": assemble,
                "g": partial_gram,
                "s": rs_mid,
                "t": rs_sum,
                "w": rs_end,
                "h": g_own,
                "k": g_far_pair,
                "f": first_prod,
                "z": second_prod,
                "o": combine,
                "v": collect,
            }[kind](*args)

    for g in (*ax, *(g for n in ay for g in n)):
        g.sent()
    for u in range(STEPS):
        wait_bytes(pbuf.at[u], sem_send.at[1, u])
    wait_bytes(gb.at[pl.ds(0, 3)], sem_send.at[2, 0])
    wait_bytes(yp.at[0, pl.ds(0, 2), pl.ds(0, 7 * 32)], sem_send.at[0, 0])
    for n, (start, width, _) in enumerate(Y_PASS):
        wait_bytes(
            fin.at[pl.ds(0, 7 * PAD), pl.ds(start, width)], sem_send.at[3 + n, 0]
        )

    @pl.when(jnp.logical_not(same))
    def _():
        wait_bytes(yp.at[0, 0, pl.ds(0, PAD)], sem_send.at[0, 1])
        for n, (start, width, _) in enumerate(Y_PASS):
            wait_bytes(
                fin.at[pl.ds(0, PAD), pl.ds(start, width)], sem_send.at[3 + n, 1]
            )


def solution(mesh):
    def step(ortho_in):
        rows, full_cols = ortho_in.shape
        full_rows = rows * mesh.size
        inv_square = 1.0 / (math.sqrt(full_rows) + math.sqrt(full_cols)) ** 2
        vmem = pltpu.VMEM
        dma = pltpu.SemaphoreType.DMA
        n = len(Y_PASS)
        parts = pl.pallas_call(
            functools.partial(kernel, inv_square),
            name="newton_schulz",
            out_shape=jax.ShapeDtypeStruct((8 * PAD, PW), BF16),
            in_specs=[pl.BlockSpec(memory_space=pl.ANY)],
            out_specs=pl.BlockSpec(memory_space=pl.ANY),
            scratch_shapes=[
                vmem((HALF, 8 * PW), BF16),
                vmem((T16, 8 * PW), BF16),
                vmem((8, T16, PW), BF16),
                vmem((STEPS, 4, SEG, PW), BF16),
                vmem((STEPS, 4, SEG, PW), BF16),
                vmem((STEPS, 2, 4, ROWS, UNIT), BF16),
                vmem((STEPS, 2, 3, ROWS, UNIT), BF16),
                vmem((STEPS, 2, ROWS, UNIT), BF16),
                vmem((4, STEPS, ROWS, BLK), BF16),
                vmem((4 * ROWS, PW), F32),
                vmem((8 * PAD, PW), BF16),
                dma((1,)),
                dma((STEPS,)),
                dma((STEPS + 4 * n, 10)),
                dma((STEPS + 4 * n, 4)),
                dma((2 * STEPS, 4)),
                dma((STEPS, 7)),
                dma((n, 8)),
                dma((3 + n, 8)),
            ],
            compiler_params=pltpu.CompilerParams(
                collective_id=0,
                has_side_effects=True,
                vmem_limit_bytes=64 * 2**20 - 2**18,
            ),
            cost_estimate=pl.CostEstimate(
                flops=3 * 2 * 448 * 7168 * 1152,
                bytes_accessed=4 * 56 * 9216,
                transcendentals=0,
            ),
        )(ortho_in)
        parts = parts.reshape(8, PAD, PW)[:, :HALF]
        return parts.transpose(1, 0, 2).reshape(rows, full_cols)

    spec = P(("row", "col"), None)
    return jax.shard_map(
        step, mesh=mesh, in_specs=(spec,), out_specs=spec, check_vma=False
    )
```

time: 195 us -> 180 us (0.923)
  Pallas kernels: 192 us -> 178 us
    pallas_call x1, Pallas kernels: 192 us -> 178 us  [step(): pl.pallas_call(functools.partial(kernel, inv_square), name='newton_schulz...]
where the time goes in v4:
time: 180 us
  Pallas kernels  178 us (99%)
  local copies, waits for them, and re-layouts  2.39 us (1%)
    pallas_call x1, Pallas kernels, step(): pl.pallas_call(functools.partial(kernel, inv_square), name='newton_schulz...  178 us

profile of v4, /device:TPU:1, one launch (start us, length us, event | category | flops | bytes accessed | tf_op | source)
XLA Modules:
  0.0 180.3 jit_solution(14289878910534380409)
XLA Ops:
  0.0 177.9 %newton_schulz.1 = bf16[512,1152]{1,0:T(8,128)(2,1)} custom-call(bf16[56,9216]{1,0:T(8,128)(2,1)} %xin.1), custom_call_target="tpu_custom_call" | custom-call | flops 22196256768 | bytes 2064384 | tf_op jit(solution)/shard_map/newton_schulz/pallas_call | solution.py:544
  177.9 1.3 slice_bitcast_fusion
  179.2 1.1 copy.3

commit v5 on v4

--- a/solution.py
+++ b/solution.py
@@ -27,28 +27,28 @@
 UNIT = BLK // 2
 X_PASS = (0, PW, 512)
 Y_PASS = ((0, 512, 256), (512, 384, 128), (896, 256, 128))
-RELAYED = (0, 2)
+RELAYED = (2, 4)
 
 ORDER = (
-    "a0", "a1", "x0o", "x1o", "a2", "a3", "x0m", "x0q", "x0p", "a4", "a5", "x1m", "x1q", "x1p",
-    "a6", "x0r", "x2o", "x0b", "x1r", "g00", "x1b", "x3o", "g10", "x2m", "x2q", "x2p", "s00", "x0e",
-    "x1e", "s10", "g01", "x3q", "g11", "t00", "x3p", "x3m", "x2r", "x4o", "t10", "s01", "x2b",
-    "x3r", "g20", "w00", "x5o", "s11", "x3b", "g30", "w10", "t01", "x4m", "x4p", "x4q", "s20",
-    "x2e", "s30", "x5q", "w01", "g21", "t11", "x3e", "t20", "x5p", "x5m", "x6o", "x4r", "g31",
-    "t30", "s21", "x4b", "w11", "x5r", "g40", "x5b", "w20", "g50", "s31", "x6p", "x6m", "w30",
-    "x6q", "t21", "s40", "x4e", "x5e", "x6b", "s50", "g41", "g51", "w21", "t40", "x6r", "t31",
-    "t50", "g60", "x6e", "s41", "w40", "g61", "w31", "s51", "s60", "w50", "t41", "s61", "h2", "t60",
-    "w41", "h4", "t51", "t61", "w60", "h0", "i2", "w51", "h5", "j2", "w61", "h6", "f0", "y00o",
-    "i4", "j4", "i0", "y00m", "y00q", "y00p", "y10o", "j0", "y00r", "y10q", "y00b", "y10p", "i5",
-    "j5", "y10m", "y20o", "y00e", "k2", "y10b", "y20q", "y20p", "i6", "f1", "y01o", "y11o", "j6",
-    "f2", "y02o", "y10r", "y21o", "y01q", "k0", "y01p", "y01m", "y20m", "y20b", "y11m", "y11q",
-    "y11p", "y02m", "y02p", "y02q", "y10e", "y21m", "y21q", "y21p", "f3", "y03o", "z00", "y01r",
-    "y01b", "y11b", "y02r", "y11r", "z10", "y02b", "y12o", "y20r", "y21r", "y21b", "y03m", "y03p",
-    "y03q", "y13o", "y01e", "y02e", "y12m", "y11e", "z01", "y12p", "y12q", "z02", "y03b", "y12r",
-    "y20e", "y13m", "z11", "y12b", "y03r", "y22o", "y13p", "z20", "y21e", "y13q", "y23o", "y12e",
-    "z21", "y03e", "y22m", "z12", "y22p", "y22q", "y13b", "z03", "o0", "y13r", "y22r", "y23p",
-    "y23q", "y22b", "y23m", "y13e", "y23b", "y22e", "y23r", "z13", "o1", "z22", "y23e", "v0", "z23",
-    "o2", "v1", "v2",
+    "a0", "x0o", "a1", "x1o", "x0m", "a5", "x0p", "x1q", "x1p", "a6", "a4", "x1m", "x0q", "a3",
+    "a2", "x0r", "x2o", "x0b", "x1r", "g00", "x1b", "g10", "x3o", "s00", "x0e", "x2m", "x2p", "s10",
+    "x1e", "g01", "x3q", "x2q", "x3p", "g11", "x2r", "x3m", "x4o", "s01", "x3r", "g20", "t10",
+    "x2b", "x3b", "s11", "x5o", "g30", "s20", "x2e", "x4m", "x4p", "x3e", "s30", "x4q", "g21",
+    "x5q", "t00", "x5p", "g31", "x4r", "x5m", "x6o", "s21", "t11", "t20", "x5r", "g40", "x4b",
+    "x5b", "g50", "t30", "w10", "x6m", "t01", "s31", "x4e", "s40", "x6q", "x5e", "x6p", "s50",
+    "w20", "g41", "x6r", "t21", "w30", "g51", "x6b", "g60", "t31", "t50", "x6e", "s41", "w11",
+    "g61", "s51", "s60", "t40", "w21", "t41", "w31", "s61", "h1", "h2", "t51", "t61", "t60", "w40",
+    "w41", "w00", "w50", "w01", "w51", "h4", "l0", "h0", "w61", "w60", "h6", "i2", "i1", "f0",
+    "y00o", "y10o", "y20o", "i4", "y00m", "y10m", "j2", "i0", "y10p", "j4", "y00q", "y20q", "y20m",
+    "y20p", "y00p", "y00r", "l1", "i6", "f1", "y11o", "j1", "y01o", "y21o", "j0", "y10q", "y10b",
+    "y00b", "k2", "y20r", "y10r", "j6", "y11p", "y20b", "y01q", "y11q", "l2", "y01m", "k4", "f2",
+    "y02o", "y01p", "y20e", "y10e", "y11b", "y01r", "y11m", "y00e", "y11r", "y02m", "y02q", "y02p",
+    "y12o", "l3", "y01b", "f3", "y03o", "y02r", "z10", "y21p", "y02b", "y12m", "y12p", "z00",
+    "y03p", "y21m", "y12q", "y01e", "y11e", "y03q", "y03m", "y13o", "z20", "z01", "y02e", "y12b",
+    "y03b", "y03r", "y12r", "y22o", "z02", "y13p", "y13q", "y13m", "y23o", "y03e", "z11", "y22m",
+    "y22q", "y12e", "y13b", "y21q", "z03", "y13r", "y23p", "y23m", "o0", "y23q", "y22p", "y22r",
+    "y13e", "z12", "y21r", "y21b", "y23b", "y22b", "z13", "y23r", "o1", "y21e", "y22e", "y23e",
+    "z21", "z22", "z23", "o2", "v0", "v1", "v2",
 )
 
 
@@ -413,18 +413,18 @@
         g_far(b)
         g_send(gref(2, g_u(b)), cpair, b, 6)
 
-    def first_prod(t):
+    def first_prod(t, part):
         e = (0, -1, 1, 2)[t]
-        if t > 0:
+        if t > 0 and part == 0:
             for b in RELAYED:
                 wait_bytes(gref(e, b + 1 - c_x), sem_g.at[b, 3 + t])
         if t == 3:
             for b in CLASSES:
-                if b not in RELAYED:
+                if b not in RELAYED and (b == STEPS - 1) == (part == 1):
                     g_far(b)
         v = steps[t]
-        acc = zacc.at[pl.ds(0, ROWS)]
-        for u in range(STEPS):
+        acc = zacc.at[pl.ds(t * ROWS, ROWS)]
+        for u in range(STEPS - 1) if part == 0 else (STEPS - 1,):
             term = jnp.dot(
                 gb[v, u], xp[u].reshape(BLK, PW), preferred_element_type=F32
             )
@@ -432,8 +432,11 @@
                 acc[...] = term
             else:
                 acc[...] += term
-        for i in range(STEPS):
-            yp[i, v, slot_rows(my_slot), :] = acc[pl.ds(i * T16, T16), :].astype(BF16)
+        if part == 1:
+            for i in range(STEPS):
+                yp[i, v, slot_rows(my_slot), :] = acc[pl.ds(i * T16, T16), :].astype(
+                    BF16
+                )
 
     def second_prod(n, t):
         ay[n][t].here(0)
@@ -477,7 +480,7 @@
         for device, zz, kk, self_too in way_back:
             move(
                 fin.at[rows_at((zz * 2 + kk) * PAD, PAD), cols],
-                out.at[rows_at((c_x * 4 + z) * PAD, PAD), cols],
+                out.at[:, cols_at((c_x * 4 + z) * PW + Y_PASS[n][0], Y_PASS[n][1])],
                 sem_send.at[3 + n, 1 if self_too else 0],
                 sem_back.at[n, c_x * 4 + z],
                 device,
@@ -507,7 +510,8 @@
                 "w": rs_end,
                 "h": g_own,
                 "k": g_far_pair,
-                "f": first_prod,
+                "l": lambda t: first_prod(t, 0),
+                "f": lambda t: first_prod(t, 1),
                 "z": second_prod,
                 "o": combine,
                 "v": collect,
@@ -541,10 +545,10 @@
         vmem = pltpu.VMEM
         dma = pltpu.SemaphoreType.DMA
         n = len(Y_PASS)
-        parts = pl.pallas_call(
+        padded = pl.pallas_call(
             functools.partial(kernel, inv_square),
             name="newton_schulz",
-            out_shape=jax.ShapeDtypeStruct((8 * PAD, PW), BF16),
+            out_shape=jax.ShapeDtypeStruct((PAD, full_cols), BF16),
             in_specs=[pl.BlockSpec(memory_space=pl.ANY)],
             out_specs=pl.BlockSpec(memory_space=pl.ANY),
             scratch_shapes=[
@@ -579,8 +583,7 @@
                 transcendentals=0,
             ),
         )(ortho_in)
-        parts = parts.reshape(8, PAD, PW)[:, :HALF]
-        return parts.transpose(1, 0, 2).reshape(rows, full_cols)
+        return padded[:rows]
 
     spec = P(("row", "col"), None)
     return jax.shard_map(

time: 180 us -> 174 us (0.967)
  Pallas kernels: 178 us -> 172 us
    pallas_call x1, Pallas kernels: 178 us -> 172 us  [step(): pl.pallas_call(functools.partial(kernel, inv_square), name='newton_schulz...]
    slice x0 -> x1, local copies, waits for them, and re-layouts: none -> 2.25 us  [step(): return padded[:rows]]
where the time goes in v5:
time: 174 us
  Pallas kernels  172 us (99%)
  local copies, waits for them, and re-layouts  2.25 us (1%)
    pallas_call x1, Pallas kernels, step(): pl.pallas_call(functools.partial(kernel, inv_square), name='newton_schulz...  172 us

profile of v5, /device:TPU:1, one launch (start us, length us, event | category | flops | bytes accessed | tf_op | source)
XLA Modules:
  0.0 174.1 jit_solution(16522689115794185530)
XLA Ops:
  0.0 171.9 %newton_schulz.1 = bf16[64,9216]{1,0:T(8,128)(2,1)} custom-call(bf16[56,9216]{1,0:T(8,128)(2,1)} %xin.1), custom_call_target="tpu_custom_call" | custom-call | flops 22196256768 | bytes 2064384 | tf_op jit(solution)/shard_map/newton_schulz/pallas_call | solution.py:548
  171.9 2.2 %slice.3 = bf16[56,9216]{1,0:T(8,128)(2,1)} slice(bf16[64,9216]{1,0:T(8,128)(2,1)} %newton_schulz.1), slice={[0:56], [0:9216]} | slice | bytes 2064384 | tf_op jit(solution)/shard_map/slice | solution.py:586

commit v6 on v5

--- a/solution.py
+++ b/solution.py
@@ -30,24 +30,24 @@
 RELAYED = (2, 4)
 
 ORDER = (
-    "a0", "x0o", "a1", "x1o", "x0m", "a5", "x0p", "x1q", "x1p", "a6", "a4", "x1m", "x0q", "a3",
-    "a2", "x0r", "x2o", "x0b", "x1r", "g00", "x1b", "g10", "x3o", "s00", "x0e", "x2m", "x2p", "s10",
-    "x1e", "g01", "x3q", "x2q", "x3p", "g11", "x2r", "x3m", "x4o", "s01", "x3r", "g20", "t10",
-    "x2b", "x3b", "s11", "x5o", "g30", "s20", "x2e", "x4m", "x4p", "x3e", "s30", "x4q", "g21",
-    "x5q", "t00", "x5p", "g31", "x4r", "x5m", "x6o", "s21", "t11", "t20", "x5r", "g40", "x4b",
-    "x5b", "g50", "t30", "w10", "x6m", "t01", "s31", "x4e", "s40", "x6q", "x5e", "x6p", "s50",
-    "w20", "g41", "x6r", "t21", "w30", "g51", "x6b", "g60", "t31", "t50", "x6e", "s41", "w11",
-    "g61", "s51", "s60", "t40", "w21", "t41", "w31", "s61", "h1", "h2", "t51", "t61", "t60", "w40",
-    "w41", "w00", "w50", "w01", "w51", "h4", "l0", "h0", "w61", "w60", "h6", "i2", "i1", "f0",
-    "y00o", "y10o", "y20o", "i4", "y00m", "y10m", "j2", "i0", "y10p", "j4", "y00q", "y20q", "y20m",
-    "y20p", "y00p", "y00r", "l1", "i6", "f1", "y11o", "j1", "y01o", "y21o", "j0", "y10q", "y10b",
-    "y00b", "k2", "y20r", "y10r", "j6", "y11p", "y20b", "y01q", "y11q", "l2", "y01m", "k4", "f2",
-    "y02o", "y01p", "y20e", "y10e", "y11b", "y01r", "y11m", "y00e", "y11r", "y02m", "y02q", "y02p",
-    "y12o", "l3", "y01b", "f3", "y03o", "y02r", "z10", "y21p", "y02b", "y12m", "y12p", "z00",
-    "y03p", "y21m", "y12q", "y01e", "y11e", "y03q", "y03m", "y13o", "z20", "z01", "y02e", "y12b",
-    "y03b", "y03r", "y12r", "y22o", "z02", "y13p", "y13q", "y13m", "y23o", "y03e", "z11", "y22m",
-    "y22q", "y12e", "y13b", "y21q", "z03", "y13r", "y23p", "y23m", "o0", "y23q", "y22p", "y22r",
-    "y13e", "z12", "y21r", "y21b", "y23b", "y22b", "z13", "y23r", "o1", "y21e", "y22e", "y23e",
+    "a1", "x1o", "a0", "a3", "x0o", "a2", "x1q", "x1p", "x1m", "x2o", "a4", "x0m", "x1r", "x2m",
+    "a5", "x3o", "x1b", "x0q", "a6", "g10", "x2p", "x0r", "x2q", "g00", "x2r", "x3q", "x4o", "s10",
+    "g20", "x1e", "x2b", "x3p", "x3m", "x3r", "s00", "g11", "x4m", "x0p", "g30", "x2e", "x3b",
+    "x4q", "s20", "x5o", "s11", "t00", "x4r", "g21", "x3e", "x0b", "x6o", "g40", "g31", "t10",
+    "x5q", "s30", "x0e", "s21", "x4p", "t20", "x5m", "t11", "g01", "x6m", "x5p", "x6q", "x5r",
+    "x6p", "w20", "s31", "g50", "s40", "x5b", "t21", "s01", "x4b", "x6r", "g60", "x5e", "x6b",
+    "t30", "x4e", "t31", "w10", "s50", "g51", "t01", "x6e", "s60", "g41", "w11", "g61", "t40",
+    "t50", "s51", "s41", "w00", "w21", "s61", "w31", "t60", "h1", "t51", "w30", "t41", "w01", "w60",
+    "h2", "w50", "t61", "w40", "w51", "w41", "h4", "l0", "h0", "w61", "h6", "i2", "f0", "y00o",
+    "y10o", "y20o", "i4", "y00p", "j2", "y10m", "j4", "i1", "y20p", "y20m", "y00q", "y00b", "y20q",
+    "i0", "y10p", "y00m", "l1", "y10q", "i6", "f1", "y01o", "j1", "y11o", "y21o", "y10r", "j6",
+    "j0", "y00r", "y10b", "k2", "y01p", "y01q", "y01m", "l2", "f2", "k4", "y11q", "y02o", "y20b",
+    "y11p", "y01r", "y00e", "y01b", "y11m", "y10e", "y20r", "y21p", "y02m", "y02q", "y02p", "y12o",
+    "l3", "f3", "y03o", "z10", "y11b", "z00", "y02r", "y11r", "y12m", "y12p", "y02b", "y03q",
+    "y03m", "y03p", "y13o", "y01e", "y20e", "z01", "y12q", "y11e", "y03r", "y22o", "y12r", "y03b",
+    "z20", "y12b", "y13p", "y13q", "y21m", "y13m", "y02e", "z11", "y23o", "y21q", "y03e", "y22m",
+    "z02", "y22q", "y12e", "y13b", "z03", "y13r", "y23p", "y23q", "y22p", "o0", "y23m", "y21r",
+    "y22r", "y21b", "y13e", "z12", "y22b", "y23b", "y23r", "z13", "o1", "y21e", "y22e", "y23e",
     "z21", "z22", "z23", "o2", "v0", "v1", "v2",
 )
 
@@ -465,27 +465,30 @@
     def combine(n):
         cols = pl.ds(Y_PASS[n][0], Y_PASS[n][1])
         gap = jnp.zeros((PAD - HALF, Y_PASS[n][1]), F32)
-        for v in range(4):
+        for j in range(0, 8, 2):
+            v = way_back[j][1]
             it = [
                 coef_a * xp[i, v, slot_rows(my_slot), cols].astype(F32)
                 + coef_b * yp[i, v, slot_rows(my_slot), cols].astype(F32)
-                + coef_c * zacc[pl.ds(v * ROWS + i * T16, T16), cols]
+                + coef_c * zacc[rows_at(v * ROWS + i * T16, T16), cols]
                 for i in range(STEPS)
             ]
             for kk in range(2):
                 mine = [it[kk], it[kk + 2], it[kk + 4], it[6][kk * 8 : kk * 8 + 8], gap]
-                fin[pl.ds((v * 2 + kk) * PAD, PAD), cols] = jnp.concatenate(
+                fin[rows_at((v * 2 + kk) * PAD, PAD), cols] = jnp.concatenate(
                     mine, axis=0
                 ).astype(BF16)
-        for device, zz, kk, self_too in way_back:
-            move(
-                fin.at[rows_at((zz * 2 + kk) * PAD, PAD), cols],
-                out.at[:, cols_at((c_x * 4 + z) * PW + Y_PASS[n][0], Y_PASS[n][1])],
-                sem_send.at[3 + n, 1 if self_too else 0],
-                sem_back.at[n, c_x * 4 + z],
-                device,
-                self_too,
-            )
+            for device, zz, kk, self_too in way_back[j : j + 2]:
+                move(
+                    fin.at[rows_at((zz * 2 + kk) * PAD, PAD), cols],
+                    out.at[
+                        :, cols_at((c_x * 4 + z) * PW + Y_PASS[n][0], Y_PASS[n][1])
+                    ],
+                    sem_send.at[3 + n, 1 if self_too else 0],
+                    sem_back.at[n, c_x * 4 + z],
+                    device,
+                    self_too,
+                )
 
     def collect(n):
         start, width, _ = Y_PASS[n]
@@ -493,7 +496,7 @@
             ref = fin.at[pl.ds(g * PAD, PAD), pl.ds(start, width)]
             wait_bytes(ref, sem_back.at[n, g])
 
-    for name in ORDER:
+    for name in [name for name in ORDER if name[0] != "v"]:
         kind, args = name[0], [int(i) for i in name[1:] if i.isdigit()]
         if kind == "x":
             getattr(ax[args[0]], name[-1])()
@@ -514,7 +517,6 @@
                 "f": lambda t: first_prod(t, 1),
                 "z": second_prod,
                 "o": combine,
-                "v": collect,
             }[kind](*args)
 
     for g in (*ax, *(g for n in ay for g in n)):
@@ -535,6 +537,9 @@
             wait_bytes(
                 fin.at[pl.ds(0, PAD), pl.ds(start, width)], sem_send.at[3 + n, 1]
             )
+
+    for n in range(len(Y_PASS)):
+        collect(n)
 
 
 def solution(mesh):

time: 174 us -> 172 us (0.989)
  Pallas kernels: 172 us -> 170 us
    pallas_call x1, Pallas kernels: 172 us -> 170 us  [step(): pl.pallas_call(functools.partial(kernel, inv_square), name='newton_schulz...]
where the time goes in v6:
time: 172 us
  Pallas kernels  170 us (99%)
  local copies, waits for them, and re-layouts  2.25 us (1%)
    pallas_call x1, Pallas kernels, step(): pl.pallas_call(functools.partial(kernel, inv_square), name='newton_schulz...  170 us

profile of v6, /device:TPU:1, one launch (start us, length us, event | category | flops | bytes accessed | tf_op | source)
XLA Modules:
  0.0 172.3 jit_solution(1357236715939267636)
XLA Ops:
  0.0 170.0 %newton_schulz.1 = bf16[64,9216]{1,0:T(8,128)(2,1)} custom-call(bf16[56,9216]{1,0:T(8,128)(2,1)} %xin.1), custom_call_target="tpu_custom_call" | custom-call | flops 22196256768 | bytes 2064384 | tf_op jit(solution)/shard_map/newton_schulz/pallas_call | solution.py:553
  170.0 2.2 %slice.3 = bf16[56,9216]{1,0:T(8,128)(2,1)} slice(bf16[64,9216]{1,0:T(8,128)(2,1)} %newton_schulz.1), slice={[0:56], [0:9216]} | slice | bytes 2064384 | tf_op jit(solution)/shard_map/slice | solution.py:591

commit v7 on v6

--- a/solution.py
+++ b/solution.py
@@ -32,18 +32,18 @@
 ORDER = (
     "a1", "x1o", "a0", "a3", "x0o", "a2", "x1q", "x1p", "x1m", "x2o", "a4", "x0m", "x1r", "x2m",
     "a5", "x3o", "x1b", "x0q", "a6", "g10", "x2p", "x0r", "x2q", "g00", "x2r", "x3q", "x4o", "s10",
-    "g20", "x1e", "x2b", "x3p", "x3m", "x3r", "s00", "g11", "x4m", "x0p", "g30", "x2e", "x3b",
-    "x4q", "s20", "x5o", "s11", "t00", "x4r", "g21", "x3e", "x0b", "x6o", "g40", "g31", "t10",
-    "x5q", "s30", "x0e", "s21", "x4p", "t20", "x5m", "t11", "g01", "x6m", "x5p", "x6q", "x5r",
-    "x6p", "w20", "s31", "g50", "s40", "x5b", "t21", "s01", "x4b", "x6r", "g60", "x5e", "x6b",
+    "x1e", "g20", "x2b", "x3p", "x3m", "x3r", "s00", "g11", "x4m", "x0p", "g30", "x2e", "x3b",
+    "x4q", "s20", "x5o", "s11", "t00", "x4r", "g21", "x3e", "x0b", "x6o", "g40", "s30", "g31",
+    "t10", "x5q", "x0e", "s21", "x4p", "t20", "x5m", "t11", "g01", "x6m", "x5p", "x6q", "x5r",
+    "x6p", "x4b", "w20", "s31", "g50", "s40", "x5b", "t21", "s01", "x6r", "g60", "x5e", "x6b",
     "t30", "x4e", "t31", "w10", "s50", "g51", "t01", "x6e", "s60", "g41", "w11", "g61", "t40",
-    "t50", "s51", "s41", "w00", "w21", "s61", "w31", "t60", "h1", "t51", "w30", "t41", "w01", "w60",
-    "h2", "w50", "t61", "w40", "w51", "w41", "h4", "l0", "h0", "w61", "h6", "i2", "f0", "y00o",
+    "s51", "w31", "w00", "t50", "w21", "s41", "s61", "t60", "h1", "w40", "t51", "t41", "w30", "h2",
+    "w50", "w01", "w60", "t61", "w51", "w41", "h4", "l0", "h0", "w61", "h6", "i2", "f0", "y00o",
     "y10o", "y20o", "i4", "y00p", "j2", "y10m", "j4", "i1", "y20p", "y20m", "y00q", "y00b", "y20q",
     "i0", "y10p", "y00m", "l1", "y10q", "i6", "f1", "y01o", "j1", "y11o", "y21o", "y10r", "j6",
-    "j0", "y00r", "y10b", "k2", "y01p", "y01q", "y01m", "l2", "f2", "k4", "y11q", "y02o", "y20b",
-    "y11p", "y01r", "y00e", "y01b", "y11m", "y10e", "y20r", "y21p", "y02m", "y02q", "y02p", "y12o",
-    "l3", "f3", "y03o", "z10", "y11b", "z00", "y02r", "y11r", "y12m", "y12p", "y02b", "y03q",
+    "y00r", "y10b", "k2", "y01p", "y01q", "j0", "y01m", "l2", "f2", "k4", "y11q", "y02o", "y11p",
+    "y01r", "y00e", "y01b", "y11m", "y10e", "y20b", "y20r", "y21p", "y02m", "y02q", "y02p", "y12o",
+    "l3", "f3", "y03o", "z10", "y11b", "z00", "y02r", "y11r", "y12p", "y12m", "y02b", "y03q",
     "y03m", "y03p", "y13o", "y01e", "y20e", "z01", "y12q", "y11e", "y03r", "y22o", "y12r", "y03b",
     "z20", "y12b", "y13p", "y13q", "y21m", "y13m", "y02e", "z11", "y23o", "y21q", "y03e", "y22m",
     "z02", "y22q", "y12e", "y13b", "z03", "y13r", "y23p", "y23q", "y22p", "o0", "y23m", "y21r",

time: 172 us -> 172 us (level)
  no operation moved by 1% of the time
where the time goes in v7:
time: 172 us
  Pallas kernels  170 us (99%)
  local copies, waits for them, and re-layouts  2.25 us (1%)
    pallas_call x1, Pallas kernels, step(): pl.pallas_call(functools.partial(kernel, inv_square), name='newton_schulz...  170 us

profile of v7, /device:TPU:1, one launch (start us, length us, event | category | flops | bytes accessed | tf_op | source)
XLA Modules:
  0.0 172.3 jit_solution(6018260285473679887)
XLA Ops:
  0.0 170.0 %newton_schulz.1 = bf16[64,9216]{1,0:T(8,128)(2,1)} custom-call(bf16[56,9216]{1,0:T(8,128)(2,1)} %xin.1), custom_call_target="tpu_custom_call" | custom-call | flops 22196256768 | bytes 2064384 | tf_op jit(solution)/shard_map/newton_schulz/pallas_call | solution.py:553
  170.0 2.2 %slice.3 = bf16[56,9216]{1,0:T(8,128)(2,1)} slice(bf16[64,9216]{1,0:T(8,128)(2,1)} %newton_schulz.1), slice={[0:56], [0:9216]} | slice | bytes 2064384 | tf_op jit(solution)/shard_map/slice | solution.py:591
